TPU v7x, 256 devices: a whole 4x4x8 slice. The times are simulated.
256 devices in a mesh: gz: 8 (over x, core), gy: 32 (over y, z).
Axes of the slice: x: 4, y: 4, z: 8, core: 2. Of those that a mesh axis runs over, the one named last changes fastest.
Arguments:
- streamwise: float32 [64, 1024, 1024], P('gz', 'gy'), may hold values from -6 to 6
- spanwise: float32 [64, 1024, 1024], P('gz', 'gy'), may hold values from -6 to 6
- wall_normal: float32 [64, 1024, 1024], P('gz', 'gy'), may hold values from -6 to 6
- spacing: float32 [64], replicated, may hold values from 0.7 to 1.4
Outputs:
- pressure: float32 [64, 1024, 1024], P('gz', 'gy')
All inputs are finite; a program needn't handle non-finite values.
Results may differ from a plain program's by a relative error of at most 0.0003.
Values sent between devices are 32-bit elements; how exact they have to be, the bound alone decides.
No kernel may reach another device: no remote copies, remote signals or barrier semaphores. Data moves between devices by JAX's collectives and lax.ppermute only.
A program may use at most 64 MiB of HBM per device.

v0:
```python
import math

import jax
import jax.numpy as jnp
from jax import lax
from jax.sharding import PartitionSpec as P

screening = 0.0015


def shifted(block, axis, distance):
    devices = range(lax.axis_size(axis))
    route = [((i - distance) % len(devices), i) for i in devices]
    return lax.ppermute(block, axis, route)


def shifted_2(shard, axis, by):
    length = lax.axis_size(axis)
    pairs = [(i, i + by) for i in range(length) if 0 <= i + by < length]
    return lax.ppermute(shard, axis, pairs)


def basis(count):
    positions = jnp.arange(count, dtype=jnp.int32)[:, None]
    columns = jnp.arange(count, dtype=jnp.int32)[None, :]
    halfway = count // 2
    waves = jnp.where(columns <= halfway, columns, columns - halfway)
    phases = positions * waves % count
    angles = 2.0 * math.pi / count * phases.astype(jnp.float32)
    scaling = jnp.where((columns == 0) | (columns == halfway), 1.0, math.sqrt(2.0)) / math.sqrt(
        count
    )
    return jnp.where(columns <= halfway, jnp.cos(angles), jnp.sin(angles)) * scaling


def eigen_values(count, wave_index):
    halfway = count // 2
    waves = jnp.where(wave_index <= halfway, wave_index, wave_index - halfway)
    return 2.0 - 2.0 * jnp.cos(2.0 * math.pi / count * waves.astype(jnp.float32))


def wall_coefficients(spacing):
    gap = 0.5 * (spacing[:-1] + spacing[1:])
    nothing = jnp.zeros((1,), jnp.float32)
    lower = jnp.concatenate([nothing, 1.0 / (gap * spacing[1:])])
    upper = jnp.concatenate([1.0 / (gap * spacing[:-1]), nothing])
    return (lower, upper)


def combine(own, lows, highs):
    left_coef, right_coef, values = own
    pivot = 1.0 / (1.0 - left_coef * lows[1] - right_coef * highs[0])
    new_left = -pivot * left_coef * lows[0]
    new_right = -pivot * right_coef * highs[1]
    new_values = pivot * (values - left_coef * lows[2] - right_coef * highs[2])
    return (new_left, new_right, new_values)


def reduce_lines(system):
    count = system[0].shape[0]
    stride = 1
    while stride < count:
        filler = jnp.zeros((stride,) + system[0].shape[1:], jnp.float32)
        lows = tuple(
            (jnp.concatenate([filler, member[: count - stride]], axis=0) for member in system)
        )
        highs = tuple((jnp.concatenate([member[stride:], filler], axis=0) for member in system))
        system = combine(system, lows, highs)
        stride = stride * 2
    return system[2]


def on_device(streamwise, spanwise, wall_normal, spacing):
    highest = lax.Precision.HIGHEST
    depth_cells, span_cells, length_x = streamwise.shape
    groups_y = lax.axis_size("gy")
    length_y = span_cells * groups_y
    lower_all, upper_all = wall_coefficients(spacing)
    first_layer = lax.axis_index("gz") * depth_cells
    heights = lax.dynamic_slice_in_dim(spacing, first_layer, depth_cells, 0)
    span_edge = shifted(spanwise[:, span_cells - 1 :, :], "gy", 1)
    span_prev = jnp.concatenate([span_edge, spanwise[:, :-1, :]], axis=1)
    wall_edge = shifted_2(wall_normal[depth_cells - 1 :], "gz", 1)
    wall_prev = jnp.concatenate([wall_edge, wall_normal[:-1]], axis=0)
    diverge = streamwise - jnp.roll(streamwise, 1, axis=2) + (spanwise - span_prev)
    diverge = diverge + (wall_normal - wall_prev) / heights[:, None, None]
    table_x = basis(length_x)
    table_y = basis(length_y)
    modes_here = length_x // groups_y
    lower = lax.dynamic_slice_in_dim(lower_all, first_layer, depth_cells, 0)
    upper = lax.dynamic_slice_in_dim(upper_all, first_layer, depth_cells, 0)
    along_x = jnp.einsum("zyx,xm->ymz", diverge, table_x, precision=highest)
    along_x = along_x.reshape(span_cells, length_x * depth_cells)
    spectral = lax.all_to_all(along_x, "gy", split_axis=1, concat_axis=0, tiled=True)
    spectral = spectral.reshape(length_y, modes_here, depth_cells)
    forcing = -jnp.einsum("yqz,yk->zqk", spectral, table_y, precision=highest)
    waves_x = lax.axis_index("gy") * modes_here + jnp.arange(modes_here, dtype=jnp.int32)
    offset = (
        eigen_values(length_x, waves_x)[:, None]
        + eigen_values(length_y, jnp.arange(length_y, dtype=jnp.int32))[None, :]
        + screening
    )
    left_list = []
    right_list = []
    value_list = []
    for height in range(depth_cells):
        low_coef = -lower[height]
        up_coef = -upper[height]
        diagonal = lower[height] + upper[height] + offset
        if height < 2:
            inverse = 1.0 / diagonal
            left_list.append(low_coef * inverse)
            right_list.append(up_coef * inverse)
            value_list.append(forcing[height] * inverse)
        else:
            inverse = 1.0 / (diagonal - low_coef * right_list[height - 1])
            value_list.append(inverse * (forcing[height] - low_coef * value_list[height - 1]))
            left_list.append(-inverse * low_coef * left_list[height - 1])
            right_list.append(inverse * up_coef)
    for height in range(depth_cells - 3, 0, -1):
        value_list[height] = value_list[height] - right_list[height] * value_list[height + 1]
        left_list[height] = left_list[height] - right_list[height] * left_list[height + 1]
        right_list[height] = -right_list[height] * right_list[height + 1]
    inverse = 1.0 / (1.0 - right_list[0] * left_list[1])
    value_list[0] = inverse * (value_list[0] - right_list[0] * value_list[1])
    left_list[0] = inverse * left_list[0]
    right_list[0] = -inverse * right_list[0] * right_list[1]
    last_cell = depth_cells - 1
    own_ends = (
        jnp.stack([left_list[0], left_list[last_cell]]),
        jnp.stack([right_list[0], right_list[last_cell]]),
        jnp.stack([value_list[0], value_list[last_cell]]),
    )
    gathered = (
        lax.all_gather(own_ends[0], "gz", axis=0, tiled=True),
        lax.all_gather(own_ends[1], "gz", axis=0, tiled=True),
        lax.all_gather(own_ends[2], "gz", axis=0, tiled=True),
    )
    solved_all = reduce_lines(gathered)
    ends = lax.dynamic_slice_in_dim(solved_all, 2 * lax.axis_index("gz"), 2, 0)
    first_value = ends[0]
    last_value = ends[1]
    layers = [first_value]
    for height in range(1, last_cell):
        layers.append(
            value_list[height] - left_list[height] * first_value - right_list[height] * last_value
        )
    layers.append(last_value)
    solved = jnp.stack(layers)
    back_y = jnp.einsum("zqk,yk->yqz", solved, table_y, precision=highest)
    back_y = back_y.reshape(length_y, modes_here * depth_cells)
    physical = lax.all_to_all(back_y, "gy", split_axis=0, concat_axis=1, tiled=True)
    physical = physical.reshape(span_cells, length_x, depth_cells)
    pressure = jnp.einsum("ymz,xm->zyx", physical, table_x, precision=highest)
    return pressure


def solution(mesh):
    placed = (P("gz", "gy", None), P("gz", "gy", None), P("gz", "gy", None), P())
    return jax.shard_map(
        on_device, mesh=mesh, in_specs=placed, out_specs=P("gz", "gy", None), check_vma=False
    )
```

profile of v0, /device:TPU:32, one launch (start us, length us, event | category | flops | bytes accessed | tf_op | source)
XLA Modules:
  0.0 274.3 jit_solution(15931421236965368233)
XLA Ops:
  6.5 0.8 multiply_divide_fusion
  7.6 0.7 fusion.98
  9.0 0.7 fusion.99
  28.5 0.5 multiply_multiply_fusion
  29.0 0.7 pad_maximum_fusion.1
  29.8 1.0 slice.222
  30.8 2.0 collective-permute-start
  32.8 0.9 slice.224
  33.7 1.5 collective-permute-start.1
  36.1 0.4 multiply_multiply_fusion.2
  36.5 0.7 pad_maximum_fusion
  37.6 1.0 slice.220
  38.7 0.6 copy-done.9
  39.3 24.0 %fusion.15 = f32[32,1024,8]{1,0,2:T(8,128)S(1)} fusion(f32[1024]{0:T(1024)S(1)} %select_multiply_fusion.5, s32[1024]{0:T(1024)S(1)} %add_select_fusion.1, pred[1024]{0:T(1024)(128)(4,1)S(1)} %iota_compare_fusion.2, f32[8,32,1024]{2,1,0:T(8,128)} %param.4, f32[8,32,1023]{2,1,0:T(8,128)} %bitcast.71, f32[8,32,1]{2,1,0:T(8,128)S(1)} %slice.220, ...), kind=kOutput, calls=%fused_computation.35 | convolution fusion | flops 3240361984 | bytes 7349280 | tf_op jit(solution)/shard_map/zyx,xm->ymz/dot_general | solution.py:92
  63.4 2.7 copy.11
  66.1 3.2 %copy.12 = f32[32,32,256]{2,0,1:T(8,128)S(1)} copy(f32[32,32,256]{0,2,1:T(8,128)} %bitcast.67) | data formatting | bytes 2097152 | tf_op jit(solution)/shard_map/all_to_all | solution.py:94
  69.3 39.5 %all_to_all.32 = f32[32,32,256]{2,0,1:T(8,128)S(1)} all-to-all(f32[32,32,256]{2,0,1:T(8,128)S(1)} %copy.12), channel_id=1, replica_groups=mesh['gz'=8,'gy'=32] {'gy'}, dimensions={1} | all-to-all | bytes 2097152 | tf_op jit(solution)/shard_map/all_to_all | solution.py:94
  108.7 4.4 %copy.13 = f32[32,32,256]{1,0,2:T(8,128)} copy(f32[32,32,256]{2,1,0:T(8,128)S(1)} %bitcast.70) | data formatting | bytes 2097152 | tf_op jit(solution)/shard_map/all_to_all | solution.py:94
  113.1 3.7 %reshape.1339 = f32[1024,32,8]{0,2,1:T(8,128)S(1)} reshape(f32[32,32,256]{1,0,2:T(8,128)} %copy.13) | data formatting | bytes 2097152 | tf_op jit(solution)/shard_map/reshape | solution.py:95
  116.9 22.5 %fusion.29 = f32[8,32,1024]{2,1,0:T(8,128)S(1)} fusion(f32[1024]{0:T(1024)S(1)} %select_multiply_fusion.5, s32[1024]{0:T(1024)S(1)} %add_select_fusion.1, pred[1024]{0:T(1024)(128)(4,1)S(1)} %iota_compare_fusion.2, f32[1024,32,8]{0,2,1:T(8,128)S(1)} %reshape.1339), kind=kOutput, calls=%fused_computation.39 | convolution fusion | flops 3238264832 | bytes 2106368 | tf_op jit(solution)/shard_map/yqz,yk->zqk/dot_general | solution.py:96
  139.4 1.1 fusion.62
  140.8 0.7 pad_maximum_fusion.2
  141.6 4.7 %fusion.97 = (f32[15,32,1024]{2,1,0:T(8,128)}, f32[15,32,1024]{2,1,0:T(8,128)}) fusion(f32[16,32,1024]{2,1,0:T(8,128)} %all-gather.6.cloned.1.call-done), kind=kLoop, calls=%fused_computation.169 | loop fusion | bytes 7864320 | tf_op jit(solution)/shard_map/slice | solution.py:65
  146.3 4.7 %fusion.96 = (f32[15,32,1024]{2,1,0:T(8,128)}, f32[15,32,1024]{2,1,0:T(8,128)}) fusion(f32[16,32,1024]{2,1,0:T(8,128)} %all-gather.4.cloned.1.call-done), kind=kLoop, calls=%fused_computation.168 | loop fusion | bytes 7864320 | tf_op jit(solution)/shard_map/slice | solution.py:65
  151.0 16.0 %all-gather.8.cloned.1.call-done = f32[16,32,1024]{2,1,0:T(8,128)} async-done(((f32[2,32,1024]{2,1,0:T(8,128)}), f32[16,32,1024]{2,1,0:T(8,128)}) %all-gather.8.cloned.1.call-update) | async-done | bytes 2097168 | tf_op jit(solution)/shard_map/all_gather | solution.py:137
  167.1 2.6 fusion.91
  169.8 0.6 copy-done.2
  170.5 4.3 %subtract_multiply_fusion.2 = (f32[16,32,1024]{2,1,0:T(8,128)S(1)}, f32[16,32,1024]{2,1,0:T(8,128)S(1)}, f32[16,32,1024]{2,1,0:T(8,128)S(1)}) fusion(f32[16,32,1024]{2,1,0:T(8,128)S(1)} %copy-done, f32[15,32,1024]{2,1,0:T(8,128)S(1)} %get-tuple-element.26, f32[16,32,1024]{2,1,0:T(8,128)S(1)} %copy-done.2, f32[16,32,1024]{2,1,0:T(8,128)S(1)} %copy-done.1, ...), kind=kLoop, calls=%fused_computation.23 | loop fusion | flops 7864320 | bytes 24379392 | tf_op jit(solution)/shard_map/mul | solution.py:55
  174.8 0.5 fusion.90
  175.3 0.5 fusion.95
  175.8 0.5 fusion.94
  176.3 2.9 %subtract_multiply_fusion.1 = (f32[16,32,1024]{2,1,0:T(8,128)S(1)}, f32[16,32,1024]{2,1,0:T(8,128)S(1)}, f32[16,32,1024]{2,1,0:T(8,128)S(1)}) fusion(f32[16,32,1024]{2,1,0:T(8,128)S(1)} %get-tuple-element.11, f32[14,32,1024]{2,1,0:T(8,128)S(1)} %get-tuple-element.24, f32[16,32,1024]{2,1,0:T(8,128)S(1)} %get-tuple-element.10, ...), kind=kLoop, calls=%fused_computation.22 | loop fusion | flops 7864320 | bytes 23592960 | tf_op jit(solution)/shard_map/mul | solution.py:55
  179.6 0.4 fusion.93
  180.0 0.4 fusion.92
  180.5 2.0 subtract_multiply_fusion
  183.1 0.4 subtract_dynamic-update-slice_fusion.5
  183.5 0.4 subtract_dynamic-update-slice_fusion.4
  183.9 0.4 subtract_dynamic-update-slice_fusion.3
  184.7 0.4 subtract_dynamic-update-slice_fusion.1
  185.5 21.0 %fusion.18 = f32[1024,32,8]{0,1,2:T(8,128)S(1)} fusion(f32[8,32,1024]{2,1,0:T(8,128)S(1)} %slice_dynamic-update-slice_fusion, f32[1024]{0:T(1024)S(1)} %select_multiply_fusion.5, s32[1024]{0:T(1024)S(1)} %add_select_fusion.1, pred[1024]{0:T(1024)(128)(4,1)S(1)} %copy-done.7), kind=kOutput, calls=%fused_computation.36 | convolution fusion | flops 3238002688 | bytes 2106368 | tf_op jit(solution)/shard_map/zqk,yk->yqz/dot_general | solution.py:150
  206.4 0.6 copy.15
  207.1 3.0 %all_to_all.27 = f32[32,32,256]{1,0,2:T(8,128)} reshape(f32[1024,32,8]{0,2,1:T(8,128)S(1)} %copy.15) | data formatting | bytes 2097152 | tf_op jit(solution)/shard_map/all_to_all | solution.py:152
  210.0 4.3 %copy.16 = f32[32,32,256]{2,1,0:T(8,128)} copy(f32[32,32,256]{1,0,2:T(8,128)} %all_to_all.27) | data formatting | bytes 2097152 | tf_op jit(solution)/shard_map/all_to_all | solution.py:152
  214.4 10.1 %all-to-all-start.1 = ((f32[32,32,256]{2,1,0:T(8,128)}), f32[32,32,256]{2,1,0:T(8,128)S(1)}, u32[]{:S(2)}, u32[]{:S(2)}) async-start(f32[32,32,256]{2,1,0:T(8,128)} %copy.16), calls=%async_computation.1 | async-start | bytes 2097152 | tf_op jit(solution)/shard_map/all_to_all | solution.py:152
  224.5 17.7 %fusion.104 = f32[1024,1024,1]{1,0,2:T(8,128)} fusion(f32[1024]{0:T(1024)S(1)} %select_multiply_fusion.5, s32[1024]{0:T(1024)S(1)} %add_select_fusion.1, pred[1024]{0:T(1024)(128)(4,1)S(1)} %copy-done.7), kind=kLoop, calls=%fused_computation.7.clone.clone.clone.1 | loop fusion | flops 16777216 | bytes 4203520 | tf_op jit(solution)/shard_map/ymz,xm->zyx/dot_general | solution.py:154
  242.2 11.0 %all-to-all-done.1 = f32[32,32,256]{2,1,0:T(8,128)S(1)} async-done(((f32[32,32,256]{2,1,0:T(8,128)}), f32[32,32,256]{2,1,0:T(8,128)S(1)}, u32[]{:S(2)}, u32[]{:S(2)}) %all-to-all-start.1) | async-done | bytes 1048608 | tf_op jit(solution)/shard_map/all_to_all | solution.py:152
  253.2 2.7 copy.17
  255.9 11.7 %fusion.21 = f32[8,32,1024]{2,1,0:T(8,128)} fusion(f32[32,1024,8]{0,2,1:T(8,128)} %bitcast.68, f32[1024,1024,1]{1,0,2:T(8,128)} %fusion.104), kind=kOutput, calls=%fused_computation.37 | convolution fusion | flops 3221225472 | bytes 6291456 | tf_op jit(solution)/shard_map/ymz,xm->zyx/dot_general | solution.py:154
  (51 shorter events, 3.6 us)
Async XLA Ops:
  6.5 31.0 %copy-start.5 = (f32[64]{0:T(128)S(1)}, f32[64]{0:T(128)}, u32[]{:S(2)}) copy-start(f32[64]{0:T(128)} %param.7) | copy-start | bytes 772
  6.5 135.1 %all-gather.6.cloned.1.call-start = ((), (), s32[]{:S(2)}) async-start(), calls=%async_computation.3 | async-start | bytes 2359296 | tf_op jit(solution)/shard_map/all_gather | solution.py:136
  29.0 10.3 %copy-start.3 = (f32[8,32,1024]{2,1,0:T(8,128)S(1)}, f32[8,32,1024]{2,1,0:T(8,128)}, u32[]{:S(2)}) copy-start(f32[8,32,1024]{2,1,0:T(8,128)} %param.6) | copy-start | bytes 3145732
  29.0 10.3 %slice-start = ((f32[8,32,1024]{2,1,0:T(8,128)}), f32[7,32,1024]{2,1,0:T(8,128)S(1)}, s32[]{:S(2)}) async-start(f32[8,32,1024]{2,1,0:T(8,128)} %param.6), calls=%async_computation.5 | async-start | bytes 1835008 | tf_op jit(solution)/shard_map/slice | solution.py:84
  29.8 116.6 %all-gather.4.cloned.1.call-start = ((), (), s32[]{:S(2)}) async-start(), calls=%async_computation.2 | async-start | bytes 2359296 | tf_op jit(solution)/shard_map/all_gather | solution.py:135
  30.8 7.8 %collective-permute-start = (f32[8,1,1024]{2,1,0:T(1,128)S(1)}, f32[8,1,1024]{2,1,0:T(1,128)S(1)}, u32[]{:S(2)}, u32[]{:S(2)}) collective-permute-start(f32[8,1,1024]{2,1,0:T(1,128)S(1)} %slice.222), channel_id=1, source_target_pairs={{31,0},{0,1},{1,2},{2,3},{3,4},{4,5},{5,6},{6,7},{7,8},{8,9},{9,10... | collective-permute-start | bytes 98312 | tf_op jit(solution)/shard_map/ppermute | solution.py:14
  33.7 4.9 %collective-permute-start.1 = (f32[1,32,1024]{2,1,0:T(8,128)S(1)}, f32[1,32,1024]{2,1,0:T(8,128)S(1)}, u32[]{:S(2)}, u32[]{:S(2)}) collective-permute-start(f32[1,32,1024]{2,1,0:T(8,128)S(1)} %slice.224), channel_id=1, source_target_pairs={{0,32},{32,64},{64,96},{96,128},{128,160},{160,192},{192,224},{1,3... | collective-permute-start | bytes 393224 | tf_op jit(solution)/shard_map/ppermute | solution.py:20
  37.3 129.8 %all-gather.8.cloned.1.call-start = ((), (), s32[]{:S(2)}) async-start(), calls=%async_computation.4 | async-start | bytes 2359296 | tf_op jit(solution)/shard_map/all_gather | solution.py:137
  37.5 79.3 %copy-start.6 = (pred[1024]{0:T(1024)(128)(4,1)}, pred[1024]{0:T(1024)(128)(4,1)S(1)}, u32[]{:S(2)}) copy-start(pred[1024]{0:T(1024)(128)(4,1)S(1)} %iota_compare_fusion.2) | copy-start | bytes 3076
  38.6 0.6 copy-start.9
  38.7 0.7 copy-start.8
  151.0 18.6 %copy-start = (f32[16,32,1024]{2,1,0:T(8,128)S(1)}, f32[16,32,1024]{2,1,0:T(8,128)}, u32[]{:S(2)}) copy-start(f32[16,32,1024]{2,1,0:T(8,128)} %all-gather.6.cloned.1.call-done) | copy-start | bytes 6291460
  167.1 2.8 %copy-start.1 = (f32[16,32,1024]{2,1,0:T(8,128)S(1)}, f32[16,32,1024]{2,1,0:T(8,128)}, u32[]{:S(2)}) copy-start(f32[16,32,1024]{2,1,0:T(8,128)} %all-gather.4.cloned.1.call-done) | copy-start | bytes 6291460
  167.1 3.4 %copy-start.2 = (f32[16,32,1024]{2,1,0:T(8,128)S(1)}, f32[16,32,1024]{2,1,0:T(8,128)}, u32[]{:S(2)}) copy-start(f32[16,32,1024]{2,1,0:T(8,128)} %all-gather.8.cloned.1.call-done) | copy-start | bytes 6291460
  182.9 1.1 copy-start.4
  183.1 2.4 copy-start.7
  214.4 38.8 %all-to-all-start.1 = ((f32[32,32,256]{2,1,0:T(8,128)}), f32[32,32,256]{2,1,0:T(8,128)S(1)}, u32[]{:S(2)}, u32[]{:S(2)}) async-start(f32[32,32,256]{2,1,0:T(8,128)} %copy.16), calls=%async_computation.1 | async-start | bytes 2097152 | tf_op jit(solution)/shard_map/all_to_all | solution.py:152
Sparse Core Ops, SparseCore 0:
  29.9 30.2 all-gather.5
  62.1 28.0 all-gather.3
  141.7 25.3 all-gather.7
where the time goes:
time: 278 us; the launch traced here: 274 us
  matrix products  79.2 us (28%)
  local copies, waits for them, and re-layouts  45.7 us (16%)
  blocking collectives  39.5 us (14%)
  other arithmetic  35.6 us (13%)
  between operations  33.5 us (12%)
  waiting for transfers between devices  27.1 us (10%)
  starting transfers between devices  13.8 us (5%)
    all_to_all x1, blocking collectives, on_device(): lax.all_to_all(along_x, 'gy', split_axis=1, concat_axis=0, tiled=True)  39.5 us
    dot_general x1, matrix products, on_device(): along_x = jnp.einsum('zyx,xm->ymz', diverge, table_x, precision=highest)  24 us
    dot_general x1, matrix products, on_device(): forcing = -jnp.einsum('yqz,yk->zqk', spectral, table_y, precision=highest)  22.5 us
    dot_general x1, matrix products, on_device(): back_y = jnp.einsum('zqk,yk->yqz', solved, table_y, precision=highest)  21 us
    dot_general x1, other arithmetic, on_device(): pressure = jnp.einsum('ymz,xm->zyx', physical, table_x, precision=highest)  17.7 us
    all_gather x1, waiting for transfers between devices, on_device(): lax.all_gather(own_ends[2], 'gz', axis=0, tiled=True)  16 us
    slice x10, local copies, waits for them, and re-layouts, reduce_lines(): member[:count - stride]  14.7 us
    dot_general x1, matrix products, on_device(): pressure = jnp.einsum('ymz,xm->zyx', physical, table_x, precision=highest)  11.7 us
  transfers between devices with their start and end apart: 6, of which 2 were waited for; matrix products, arithmetic and copies ran while one was open for 34% of the time, Pallas kernels for 0%

commit v1 on v0

v1 whole, which is shorter than its diff:
```python
import functools
import math

import jax
import jax.numpy as jnp
import ml_dtypes
import numpy as np
from jax import lax
from jax.experimental import pallas as pl
from jax.experimental.pallas import tpu as pltpu
from jax.sharding import PartitionSpec as P

screening = 0.0015
NX = 1024
NY = 1024
NZ = 64
GZ = 8
GY = 32
LZ = NZ // GZ
LY = NY // GY
DEV = GZ * GY
KX = NX // DEV
f32 = jnp.float32
bf16 = jnp.bfloat16


def basis(count):
    j = np.arange(count)[:, None]
    m = np.arange(count)[None, :]
    half = count // 2
    wave = np.where(m <= half, m, m - half)
    angle = 2.0 * np.pi / count * ((j * wave) % count)
    scale = np.where((m == 0) | (m == half), 1.0, math.sqrt(2.0)) / math.sqrt(count)
    return np.where(m <= half, np.cos(angle), np.sin(angle)) * scale


def eigen(count):
    m = np.arange(count)
    half = count // 2
    wave = np.where(m <= half, m, m - half)
    return 2.0 - 2.0 * np.cos(2.0 * np.pi / count * wave)


def two(x):
    hi = np.asarray(x, np.float64).astype(ml_dtypes.bfloat16)
    lo = (x - hi.astype(np.float64)).astype(ml_dtypes.bfloat16)
    return hi, lo


@functools.lru_cache(maxsize=None)
def tables():
    half = NX // 2
    tx = basis(NX)
    ex = eigen(NX)
    columns = [
        np.concatenate([np.arange(0, half + 1, 4), half + np.arange(4, half, 4)]),
        np.concatenate([np.arange(2, half, 4), half + np.arange(2, half, 4)]),
        np.arange(1, half, 2),
        half + np.arange(1, half, 2),
    ]
    parts = [tx[:256, columns[0]], tx[:256, columns[1]], tx[:512, columns[2]], tx[:512, columns[3]]]
    fx = np.concatenate(parts, axis=0)
    ix = np.concatenate([part.T for part in parts[:2]], axis=0)
    ix2 = np.concatenate([part.T for part in parts[2:]], axis=0)
    lam_x = np.stack([ex[c] for c in columns])

    sine = np.zeros((LY, LY))
    sine[0, 0] = 1.0
    m = np.arange(1, LY)
    sine[1:, 1:] = math.sqrt(2.0 / LY) * np.sin(np.pi * m[:, None] * m[None, :] / LY)
    mu = np.full((LY,), 2.0)
    mu[1:] = 2.0 - 2.0 * np.cos(np.pi * m / LY)
    kron = np.kron(np.eye(LZ), sine)
    off1 = lam_x[:, None, :] + mu[None, :, None] + screening
    q_first = sine[:, 1].copy()
    q_first[0] = 0.0
    q_last = sine[:, LY - 1].copy()
    q_last[0] = 0.0
    mask = np.ones((LY,))
    mask[0] = 0.0
    side = np.stack([np.repeat(v[:, None], 256, axis=1) for v in (q_first, q_last, mask)])

    ty = basis(NY)
    ey = eigen(NY)
    main = basis(GY)
    partner = np.zeros((GY, GY))
    for p in range(1, GY // 2):
        partner[:, p] = main[:, GY // 2 + p]
        partner[:, GY // 2 + p] = main[:, p]
    wave = np.where(np.arange(NY) <= NY // 2, np.arange(NY), np.arange(NY) - NY // 2)
    is_cos = np.arange(NY) <= NY // 2
    fold = wave % GY
    fold = np.minimum(fold, GY - fold)
    order = np.zeros((GY, GY), np.int64)
    for p in range(GY):
        if p in (0, GY // 2):
            order[:, p] = np.nonzero(fold == p)[0]
        elif p < GY // 2:
            order[:, p] = np.nonzero((fold == p) & is_cos)[0]
        else:
            order[:, p] = np.nonzero((fold == p - GY // 2) & ~is_cos)[0]
    shaped = ty.reshape(GY, LY, NY)[:, :, order]
    a_y = np.einsum("bvjp,bp->vjp", shaped, main)
    b_y = np.einsum("bvjp,bp->vjp", shaped, partner)
    a_m = np.einsum("mv,vjp->mjp", sine, a_y)
    b_m = np.einsum("mv,vjp->mjp", sine, b_y)
    a_m = np.tile(a_m, (1, 1, KX))
    b_m = np.tile(b_m, (1, 1, KX))
    lam_y = np.tile(ey[order], (1, KX)) + screening
    lam_d = np.repeat(lam_x.T, GY, axis=1)
    spread = np.eye(KX)
    dft = np.concatenate([np.kron(spread, main), np.kron(spread, partner)], axis=1)
    as32 = lambda x: np.ascontiguousarray(x, np.float32)
    return dict(
        fx=two(fx),
        ix=two(ix),
        ix2=two(ix2),
        kron=two(kron),
        sine=two(sine),
        off1=as32(off1),
        side=as32(side),
        dft=two(dft),
        idft=two(dft.T),
        fwd=as32(np.stack([a_m, b_m])),
        inv=as32(np.stack([a_m, b_m]).transpose(0, 2, 1, 3)),
        lam_y=as32(lam_y),
        lam_d=as32(lam_d),
    )


def split(x):
    hi = x.astype(bf16)
    return hi, (x - hi.astype(f32)).astype(bf16)


def dot(a, b):
    return lax.dot_general(a, b, (((1,), (0,)), ((), ())), preferred_element_type=f32)


def dot3(a, b):
    return dot(a[0], b[0]) + (dot(a[0], b[1]) + dot(a[1], b[0]))


def wall_rows(spacing, width):
    first = lax.axis_index("gz") * LZ
    inside = first + LZ < NZ
    heights = [jnp.full((1, width), spacing[first + t], f32) for t in range(LZ)]
    above = jnp.full((1, width), spacing[jnp.minimum(first + LZ, NZ - 1)], f32)
    heights.append(above)
    gaps = [0.5 * (heights[t] + heights[t + 1]) for t in range(LZ)]
    keep = jnp.where(inside, 1.0, 0.0).astype(f32)
    lower = [None] + [1.0 / (gaps[t - 1] * heights[t]) for t in range(1, LZ + 1)]
    upper = [1.0 / (gaps[t] * heights[t]) for t in range(LZ)]
    inverse = [1.0 / heights[t] for t in range(LZ + 1)]
    lower[LZ] = lower[LZ] * keep
    upper[LZ - 1] = upper[LZ - 1] * keep
    inverse[LZ] = inverse[LZ] * keep
    return lower, upper, inverse


def block_pivots(off, mask, lower, upper):
    pivots = [None] * LZ
    for t in range(1, LZ):
        diagonal = off + (lower[t] + upper[t])
        if t > 1:
            diagonal = diagonal - (lower[t] * upper[t - 1]) * pivots[t - 1]
        pivots[t] = mask / diagonal
    return pivots


def block_solve(right, pivots, lower, upper):
    value = [None] * LZ
    for t in range(1, LZ):
        term = right[t] if t == 1 else right[t] + lower[t] * value[t - 1]
        value[t] = term * pivots[t]
    for t in range(LZ - 2, 0, -1):
        value[t] = value[t] + upper[t] * pivots[t] * value[t + 1]
    return value


def eliminate(
    spacing, stream, span, wall, fx_hi, fx_lo, kron_hi, kron_lo, sine_hi, sine_lo, off1, side,
    message, kept, part_hi, part_lo, ends,
):
    lower, upper, inverse = wall_rows(spacing, NX)
    rows = lax.broadcasted_iota(jnp.int32, (LY, NX), 0)
    for t in range(LZ + 2):
        if t < LZ:
            u = stream[t]
            v = span[t]
            w = wall[t]
            shifted = jnp.where(rows == 0, 0.0, pltpu.roll(v, 1, axis=0))
            d = (pltpu.roll(u, 1, axis=1) - u) + (shifted - v)
            d = d - w * inverse[t] if t == 0 else d + (wall[t - 1] - w) * inverse[t]
        elif t == LZ:
            d = wall[LZ - 1] * inverse[LZ]
        else:
            d = jnp.concatenate([span[z, LY - 1 :, :] for z in range(LZ)] + [jnp.zeros((8, NX), f32)], axis=0)
        even = d[:, :512] + d[:, 512:]
        odd = d[:, :512] - d[:, 512:]
        here = pl.ds(t * LY, d.shape[0])
        for first, piece in ((0, even[:, :256] + even[:, 256:]), (256, even[:, :256] - even[:, 256:]), (512, odd)):
            hi, lo = split(piece)
            part_hi[here, first : first + piece.shape[1]] = hi
            part_lo[here, first : first + piece.shape[1]] = lo
    lower, upper, inverse = wall_rows(spacing, 256)
    q_first, q_last, mask = side[0], side[1], side[2]
    for i in range(KX):
        cols = ((0, 256), (256, 512), (512, 1024), (512, 1024))[i]
        deep = ((0, 256), (256, 512), (512, 1024), (1024, 1536))[i]
        a = (part_hi[:, cols[0] : cols[1]], part_lo[:, cols[0] : cols[1]])
        b = (fx_hi[deep[0] : deep[1], :], fx_lo[deep[0] : deep[1], :])
        lines = dot3(a, b)
        cells = dot3((kron_hi[...], kron_lo[...]), split(lines[: LZ * LY]))
        crown = dot3((sine_hi[...], sine_lo[...]), split(lines[LZ * LY : (LZ + 1) * LY]))
        edge = lines[(LZ + 1) * LY : (LZ + 1) * LY + LZ]
        kept[i] = cells
        layers = [cells[t * LY : (t + 1) * LY] for t in range(LZ)]
        pivots = block_pivots(off1[i], mask, lower, upper)
        inner = block_solve(layers, pivots, lower, upper)
        ends[i * LY : (i + 1) * LY, :] = layers[0] + upper[0] * inner[1]
        ends[128 + i * LY : 128 + (i + 1) * LY, :] = crown + lower[LZ] * inner[LZ - 1]
        own = [jnp.zeros((1, 256), f32)]
        following = [jnp.zeros((1, 256), f32)]
        for t in range(1, LZ):
            own.append(layers[t][:1] + jnp.sum(inner[t] * q_first, axis=0, keepdims=True))
            following.append(jnp.sum(inner[t] * q_last, axis=0, keepdims=True))
        ends[256 + i * LZ : 256 + (i + 1) * LZ, :] = jnp.concatenate(own, axis=0)
        ends[320 + i * LZ : 320 + (i + 1) * LZ, :] = edge + jnp.concatenate(following, axis=0)
    ends[256 + KX * LZ : 320, :] = jnp.zeros((64 - KX * LZ, 256), f32)
    ends[320 + KX * LZ : 384, :] = jnp.zeros((64 - KX * LZ, 256), f32)
    for r in range(3):
        message[pl.ds(r, DEV, stride=3), :] = ends[128 * r : 128 * (r + 1), :].T


def interface(
    spacing, arrived, dft_hi, dft_lo, idft_hi, idft_lo, fwd, inv, lam_y, lam_d,
    reply, pivot, value, low, up, spec, lines, top, back,
):
    me = lax.axis_index("gz") * GY + lax.axis_index("gy")
    for z in range(NZ):
        low[z : z + 1, :] = jnp.full((1, 128), spacing[z], f32)
    heights = low[...]
    layer = lax.broadcasted_iota(jnp.int32, (NZ, 128), 0)
    gap = 0.5 * (heights + pltpu.roll(heights, NZ - 1, axis=0))
    upper_all = jnp.where(layer == NZ - 1, 0.0, 1.0 / (gap * heights))
    lower_all = jnp.where(layer == 0, 0.0, 1.0 / (pltpu.roll(gap, 1, axis=0) * heights))
    low[...] = lower_all
    up[...] = upper_all
    off = lam_y[...] + lam_d[pl.ds(me, 1), :]
    half = NZ // 2
    for s in range(half):
        for z in (s, NZ - 1 - s):
            diagonal = off + (low[z : z + 1, :] + up[z : z + 1, :])
            if s > 0:
                if z < half:
                    cross = low[z : z + 1, :] * up[z - 1 : z, :]
                    diagonal = diagonal - cross * pivot[z - 1]
                else:
                    cross = up[z : z + 1, :] * low[z + 1 : z + 2, :]
                    diagonal = diagonal - cross * pivot[z + 1]
            pivot[z] = 1.0 / diagonal
    lane = lax.broadcasted_iota(jnp.int32, (GY, 128), 1)
    field = [arrived[pl.ds(96 * a, GY, stride=3), :] for a in range(GZ)]
    for a in range(1, GZ):
        field[a] = field[a] + arrived[pl.ds(96 * (a - 1) + 1, GY, stride=3), :]
    for g in range(2):
        blocks = []
        for i in range(KX):
            block = None
            for k in range(4):
                moved = pltpu.roll(field[4 * g + k], (32 * (k - i)) % 128, axis=1)
                block = moved if block is None else jnp.where(lane // 32 == k, moved, block)
            blocks.append(block)
        stacked = jnp.concatenate(blocks, axis=0).T
        spec[128 * g : 128 * (g + 1), :] = dot3(split(stacked), (dft_hi[...], dft_lo[...]))
    sides = []
    for a in range(GZ):
        rest = arrived[pl.ds(96 * a + 2, GY, stride=3), :]
        sides.append(rest + pltpu.roll(pltpu.roll(rest, 64, axis=1), 1, axis=0))
    blocks = []
    for i in range(KX):
        block = jnp.zeros((GY, 128), f32)
        for a in range(GZ):
            moved = pltpu.roll(sides[a], (8 * (a - i)) % 128, axis=1)
            block = jnp.where(lane // 8 == a, moved, block)
        blocks.append(block)
    stacked = jnp.concatenate(blocks, axis=0).T[:NZ]
    lines[...] = dot3(split(stacked), (dft_hi[:, :128], dft_lo[:, :128]))
    for g in range(2):
        total = [jnp.zeros((GY, 128), f32)] * 4
        for m in range(LY):
            c_main = fwd[0, m]
            c_partner = fwd[1, m]
            for k in range(4):
                row = 128 * g + 32 * k + m
                total[k] = total[k] + c_main * spec[row : row + 1, :128] + c_partner * spec[row : row + 1, 128:]
        for k in range(4):
            top[4 * g + k] = total[k]
    weight = fwd[0, 0]
    for s in range(half):
        for z in (s, NZ - 1 - s):
            right = weight * lines[z : z + 1, :]
            if z % LZ == 0:
                right = right + top[z // LZ]
            if s > 0:
                if z < half:
                    right = right + low[z : z + 1, :] * value[z - 1]
                else:
                    right = right + up[z : z + 1, :] * value[z + 1]
            value[z] = right * pivot[z]
    alpha = up[half - 1 : half, :] * pivot[half - 1]
    beta = low[half : half + 1, :] * pivot[half]
    below = (value[half - 1] + alpha * value[half]) / (1.0 - alpha * beta)
    above = value[half] + beta * below
    for s in range(half):
        for z in (half - 1 - s, half + s):
            if z < half:
                if s > 0:
                    below = value[z] + up[z : z + 1, :] * pivot[z] * below
                now = below
            else:
                if s > 0:
                    above = value[z] + low[z : z + 1, :] * pivot[z] * above
                now = above
            lines[z : z + 1, :] = jnp.sum(now * weight, axis=0, keepdims=True)
            if z % LZ == 0:
                top[z // LZ] = now
    for g in range(2):
        total = [jnp.zeros((LY, 128), f32)] * 4
        other = [jnp.zeros((LY, 128), f32)] * 4
        for j in range(GY):
            c_main = inv[0, j]
            c_partner = inv[1, j]
            for k in range(4):
                row = top[4 * g + k, j : j + 1, :]
                total[k] = total[k] + c_main * row
                other[k] = other[k] + c_partner * row
        for k in range(4):
            spec[128 * g + 32 * k : 128 * g + 32 * (k + 1), :128] = total[k]
            spec[128 * g + 32 * k : 128 * g + 32 * (k + 1), 128:] = other[k]
    for g in range(2):
        back[...] = dot3(split(spec[128 * g : 128 * (g + 1), :]), (idft_hi[...], idft_lo[...])).T
        for k in range(4):
            block = None
            for i in range(KX):
                moved = pltpu.roll(back[32 * i : 32 * (i + 1), :], (32 * (i - k)) % 128, axis=1)
                block = moved if block is None else jnp.where(lane // 32 == i, moved, block)
            a = 4 * g + k
            reply[pl.ds(96 * a, GY, stride=3), :] = block
            if a > 0:
                reply[pl.ds(96 * (a - 1) + 1, GY, stride=3), :] = block
    reply[pl.ds(96 * (GZ - 1) + 1, GY, stride=3), :] = jnp.zeros((GY, 128), f32)
    rest = dot3(split(lines[...]), (idft_hi[:128, :], idft_lo[:128, :]))
    back[...] = jnp.concatenate([rest, rest], axis=0).T
    pieces = []
    for i in range(KX):
        piece = back[32 * i : 32 * (i + 1), :]
        pieces.append(jnp.where(lane < 64, piece, pltpu.roll(piece, GY - 1, axis=0)))
    for a in range(GZ):
        block = jnp.zeros((GY, 128), f32)
        for i in range(KX):
            moved = pltpu.roll(pieces[i], (8 * (i - a)) % 128, axis=1)
            block = jnp.where((lane % 64) // 8 == i, moved, block)
        reply[pl.ds(96 * a + 2, GY, stride=3), :] = block


def restore(
    spacing, arrived, kept, ix_hi, ix_lo, ix2_hi, ix2_lo, kron_hi, kron_lo, off1, side, pressure, ends,
):
    lower, upper, _ = wall_rows(spacing, 256)
    q_first, q_last, mask = side[0], side[1], side[2]
    for r in range(3):
        ends[128 * r : 128 * (r + 1), :] = arrived[pl.ds(r, DEV, stride=3), :].T
    halves = []
    odd = None
    for i in range(KX):
        floor = ends[i * LY : (i + 1) * LY, :]
        ceiling = ends[128 + i * LY : 128 + (i + 1) * LY, :]
        pivots = block_pivots(off1[i], mask, lower, upper)
        right = [None] * LZ
        near = [None] * LZ
        for t in range(1, LZ):
            near[t] = ends[256 + i * LZ + t : 256 + i * LZ + t + 1, :]
            far = ends[320 + i * LZ + t : 320 + i * LZ + t + 1, :]
            right[t] = kept[i, t * LY : (t + 1) * LY, :] + (q_first * near[t] + q_last * far)
        right[1] = right[1] + lower[1] * floor
        right[LZ - 1] = right[LZ - 1] + upper[LZ - 1] * ceiling
        inner = block_solve(right, pivots, lower, upper)
        layers = [floor] + [inner[t] + (1.0 - mask) * near[t] for t in range(1, LZ)]
        modes = jnp.concatenate(layers, axis=0)
        lines = split(dot3((kron_hi[...], kron_lo[...]), split(modes)))
        if i < 2:
            halves.append(dot3(lines, (ix_hi[256 * i : 256 * (i + 1), :], ix_lo[256 * i : 256 * (i + 1), :])))
        else:
            k = i - 2
            term = dot3(lines, (ix2_hi[256 * k : 256 * (k + 1), :], ix2_lo[256 * k : 256 * (k + 1), :]))
            odd = term if odd is None else odd + term
    first = halves[0] + halves[1]
    second = halves[0] - halves[1]
    for q, piece in ((0, first + odd[:, :256]), (1, second + odd[:, 256:]), (2, first - odd[:, :256]), (3, second - odd[:, 256:])):
        for t in range(LZ):
            pressure[t, :, 256 * q : 256 * (q + 1)] = piece[t * LY : (t + 1) * LY, :]


def on_device(streamwise, spanwise, wall_normal, spacing):
    table = tables()
    as_array = lambda name: [jnp.asarray(part) for part in table[name]]
    smem = pl.BlockSpec(memory_space=pltpu.SMEM)
    vmem = pl.BlockSpec(memory_space=pltpu.VMEM)
    params = pltpu.CompilerParams(vmem_limit_bytes=50 * 2**20)
    shape = jax.ShapeDtypeStruct
    fx, ix, ix2, kron, sine = (as_array(name) for name in ("fx", "ix", "ix2", "kron", "sine"))
    dft, idft = as_array("dft"), as_array("idft")
    off1, side, fwd, inv, lam_y, lam_d = (
        jnp.asarray(table[name]) for name in ("off1", "side", "fwd", "inv", "lam_y", "lam_d")
    )
    message, kept = pl.pallas_call(
        eliminate,
        out_shape=(shape((3 * DEV, 128), f32), shape((KX, LZ * LY, 256), f32)),
        in_specs=[smem] + [vmem] * 11,
        out_specs=(vmem, vmem),
        scratch_shapes=[
            pltpu.VMEM(((LZ + 1) * LY + 16, NX), bf16),
            pltpu.VMEM(((LZ + 1) * LY + 16, NX), bf16),
            pltpu.VMEM((384, 256), f32),
        ],
        compiler_params=params,
        name="eliminate",
    )(spacing, streamwise, spanwise, wall_normal, *fx, *kron, *sine, off1, side)
    axes = ("gz", "gy")
    trade = lambda x: lax.all_to_all(
        x.reshape(DEV, 1, 384), axes, split_axis=0, concat_axis=0, tiled=True
    ).reshape(3 * DEV, 128)
    arrived = trade(message)
    reply = pl.pallas_call(
        interface,
        out_shape=shape((3 * DEV, 128), f32),
        in_specs=[smem] + [vmem] * 9,
        out_specs=vmem,
        scratch_shapes=[
            pltpu.VMEM((NZ, GY, 128), f32),
            pltpu.VMEM((NZ, GY, 128), f32),
            pltpu.VMEM((NZ, 128), f32),
            pltpu.VMEM((NZ, 128), f32),
            pltpu.VMEM((256, 256), f32),
            pltpu.VMEM((NZ, 128), f32),
            pltpu.VMEM((GZ, GY, 128), f32),
            pltpu.VMEM((128, 128), f32),
        ],
        compiler_params=params,
        name="interface",
    )(spacing, arrived, *dft, *idft, fwd, inv, lam_y, lam_d)
    answered = trade(reply)
    return pl.pallas_call(
        restore,
        out_shape=shape((LZ, LY, NX), f32),
        in_specs=[smem] + [vmem] * 10,
        out_specs=vmem,
        scratch_shapes=[pltpu.VMEM((384, 256), f32)],
        compiler_params=params,
        name="restore",
    )(spacing, answered, kept, *ix, *ix2, *kron, off1, side)


def solution(mesh):
    placed = (P("gz", "gy", None), P("gz", "gy", None), P("gz", "gy", None), P())
    return jax.shard_map(
        on_device, mesh=mesh, in_specs=placed, out_specs=P("gz", "gy", None), check_vma=False
    )
```

time: 278 us -> 78 us (0.28)
  the two profiles are of different devices: /device:TPU:32 before, /device:TPU:1 now
where the time goes in v1:
time: 78 us; the launch traced here: 77.6 us
  blocking collectives  57.6 us (74%)
  Pallas kernels  12.4 us (16%)
  local copies, waits for them, and re-layouts  7.34 us (9%)
    all_to_all x2, blocking collectives, on_device(): lax.all_to_all(x.reshape(DEV, 1, 384), axes, split_axis=0, concat_axis=0,...  57.6 us
    unnamed x50, local copies, waits for them, and re-layouts  7.34 us
    pallas_call x1, Pallas kernels, on_device(): pl.pallas_call(eliminate, out_shape=(shape((3 * DEV, 128), f32), shape((K...  5.09 us
    pallas_call x1, Pallas kernels, on_device(): pl.pallas_call(restore, out_shape=shape((LZ, LY, NX), f32), in_specs=[sme...  3.72 us
    pallas_call x1, Pallas kernels, on_device(): pl.pallas_call(interface, out_shape=shape((3 * DEV, 128), f32), in_specs=...  3.58 us

profile of v1, /device:TPU:1, one launch (start us, length us, event | category | flops | bytes accessed | tf_op | source)
XLA Modules:
  0.0 77.6 jit_solution(14805374964407670117)
XLA Ops:
  0.0 0.0 copy-start.23
  0.0 0.0 copy-start.22
  0.0 0.7 copy-done.23
  0.7 0.0 copy-done.22
  0.7 0.0 copy-start.2
  0.7 1.1 %copy-done.2 = bf16[1536,256]{1,0:T(8,128)(2,1)S(1)} copy-done((bf16[1536,256]{1,0:T(8,128)(2,1)S(1)}, bf16[1536,256]{1,0:T(8,128)(2,1)}, u32[]{:S(2)}) %copy-start.2) | copy-done | bytes 786456
  1.8 0.0 copy-start.3
  1.9 1.1 %copy-done.3 = bf16[1536,256]{1,0:T(8,128)(2,1)S(1)} copy-done((bf16[1536,256]{1,0:T(8,128)(2,1)S(1)}, bf16[1536,256]{1,0:T(8,128)(2,1)}, u32[]{:S(2)}) %copy-start.3) | copy-done | bytes 786456
  3.0 0.9 %copy-done.6 = f32[4,32,256]{2,1,0:T(8,128)S(1)} copy-done((f32[4,32,256]{2,1,0:T(8,128)S(1)}, f32[4,32,256]{2,1,0:T(8,128)}, u32[]{:S(2)}) %copy-start.6) | copy-done | bytes 131096
  3.9 0.9 %copy-done.8 = bf16[256,256]{1,0:T(8,128)(2,1)S(1)} copy-done((bf16[256,256]{1,0:T(8,128)(2,1)S(1)}, bf16[256,256]{1,0:T(8,128)(2,1)}, u32[]{:S(2)}) %copy-start.8) | copy-done | bytes 131096
  4.8 0.9 %copy-done.10 = bf16[256,256]{1,0:T(8,128)(2,1)S(1)} copy-done((bf16[256,256]{1,0:T(8,128)(2,1)S(1)}, bf16[256,256]{1,0:T(8,128)(2,1)}, u32[]{:S(2)}) %copy-start.10) | copy-done | bytes 131096
  5.7 0.9 %copy-done.12 = f32[3,32,256]{2,1,0:T(8,128)S(1)} copy-done((f32[3,32,256]{2,1,0:T(8,128)S(1)}, f32[3,32,256]{2,1,0:T(8,128)}, u32[]{:S(2)}) %copy-start.12) | copy-done | bytes 98328
  6.6 0.7 copy-done.24
  7.2 5.1 %eliminate.1 = (f32[768,128]{1,0:T(8,128)S(1)}, f32[4,256,256]{2,1,0:T(8,128)S(1)}) custom-call(f32[64]{0:T(128)S(1)} %copy-done.24, f32[8,32,1024]{2,1,0:T(8,128)} %stream.1, f32[8,32,1024]{2,1,0:T(8,128)} %span.1, f32[8,32,1024]{2,1,0:T(8,128)} %wall.1, bf16[1536,256]{1,0:T(8,128)(2,1)S(1)} %copy-done.3, bf16[1536,256]{1,0:T(8,128)(2,1)S(1)} %copy-done.2, ...), custom_call_target="tpu_custom_call" | custom-call | tf_op jit(solution)/shard_map/eliminate/pallas_call | solution.py:418
  12.3 0.0 copy-start.16
  12.4 0.0 copy-start.17
  12.4 0.0 copy-start.18
  12.4 0.0 copy-start.19
  12.4 0.0 copy-start.20
  12.4 0.0 copy-start.21
  12.4 33.8 %all_to_all.10 = f32[256,1,384]{2,1,0:T(1,128)S(1)} all-to-all(f32[256,1,384]{2,1,0:T(1,128)S(1)} %bitcast.7), channel_id=1, replica_groups=mesh['gz'=8,'gy'=32] {'gz','gy'}, dimensions={0} | all-to-all | bytes 786432 | tf_op jit(solution)/shard_map/all_to_all | solution.py:432
  46.3 0.0 copy-done
  46.3 0.0 copy-done.1
  46.3 0.0 copy-done.16
  46.3 0.0 copy-done.17
  46.3 0.0 copy-done.18
  46.3 0.0 copy-done.19
  46.3 0.0 copy-done.20
  46.3 0.0 copy-done.21
  46.3 0.0 copy-start.5
  46.3 0.0 copy-start.11
  46.4 0.0 copy-start.13
  46.4 0.0 copy-start.14
  46.4 0.0 copy-start.15
  46.4 3.6 %interface.1 = f32[768,128]{1,0:T(8,128)S(1)} custom-call(f32[64]{0:T(128)S(1)} %copy-done.24, f32[768,128]{1,0:T(8,128)S(1)} %bitcast.5, bf16[128,256]{1,0:T(8,128)(2,1)S(1)} %copy-done.20, bf16[128,256]{1,0:T(8,128)(2,1)S(1)} %copy-done.19, bf16[256,128]{1,0:T(8,128)(2,1)S(1)} %copy-done.18, bf16[256,128]{1,0:T(8,128)(2,1)S(1)} %copy-done.17, ...), custom_call_target="tpu_custom_call" | custom-call | tf_op jit(solution)/shard_map/interface/pallas_call | solution.py:436
  50.0 0.0 copy-start.4
  50.0 0.0 copy-start.7
  50.0 0.0 copy-start.9
  50.0 23.8 %all_to_all.11 = f32[256,1,384]{2,1,0:T(1,128)S(1)} all-to-all(f32[256,1,384]{2,1,0:T(1,128)S(1)} %bitcast.6), channel_id=1, replica_groups=mesh['gz'=8,'gy'=32] {'gz','gy'}, dimensions={0} | all-to-all | bytes 786432 | tf_op jit(solution)/shard_map/all_to_all | solution.py:432
  73.8 0.0 copy-done.5
  73.8 0.0 copy-done.11
  73.8 0.0 copy-done.13
  73.8 0.0 copy-done.14
  73.8 0.0 copy-done.15
  73.8 0.0 copy-done.4
  73.9 0.0 copy-done.7
  73.9 0.0 copy-done.9
  73.9 3.7 %restore.1 = f32[8,32,1024]{2,1,0:T(8,128)} custom-call(f32[64]{0:T(128)S(1)} %copy-done.24, f32[768,128]{1,0:T(8,128)S(1)} %bitcast.4, f32[4,256,256]{2,1,0:T(8,128)S(1)} %get-tuple-element.8.kept, bf16[512,256]{1,0:T(8,128)(2,1)S(1)} %copy-done.15, bf16[512,256]{1,0:T(8,128)(2,1)S(1)} %copy-done.14, bf16[512,512]{1,0:T(8,128)(2,1)S(1)} %copy-done.5, ...), custom_call_target="tpu_custom_call" | custom-call | tf_op jit(solution)/shard_map/restore/pallas_call | solution.py:455
  (7 shorter events, 0.0 us)
Async XLA Ops:
  0.0 0.7 copy-start.23
  0.0 0.7 copy-start.22
  0.7 1.1 %copy-start.2 = (bf16[1536,256]{1,0:T(8,128)(2,1)S(1)}, bf16[1536,256]{1,0:T(8,128)(2,1)}, u32[]{:S(2)}) copy-start(bf16[1536,256]{1,0:T(8,128)(2,1)} %constant.41.clone.fx_lo) | copy-start | bytes 2359300
  1.8 1.1 %copy-start.3 = (bf16[1536,256]{1,0:T(8,128)(2,1)S(1)}, bf16[1536,256]{1,0:T(8,128)(2,1)}, u32[]{:S(2)}) copy-start(bf16[1536,256]{1,0:T(8,128)(2,1)} %constant.40.clone.fx_hi) | copy-start | bytes 2359300
  3.0 0.9 %copy-start.6 = (f32[4,32,256]{2,1,0:T(8,128)S(1)}, f32[4,32,256]{2,1,0:T(8,128)}, u32[]{:S(2)}) copy-start(f32[4,32,256]{2,1,0:T(8,128)} %constant.54.clone.off1) | copy-start | bytes 393220
  3.9 0.9 %copy-start.8 = (bf16[256,256]{1,0:T(8,128)(2,1)S(1)}, bf16[256,256]{1,0:T(8,128)(2,1)}, u32[]{:S(2)}) copy-start(bf16[256,256]{1,0:T(8,128)(2,1)} %constant.47.clone.kron_lo) | copy-start | bytes 393220
  4.8 0.9 %copy-start.10 = (bf16[256,256]{1,0:T(8,128)(2,1)S(1)}, bf16[256,256]{1,0:T(8,128)(2,1)}, u32[]{:S(2)}) copy-start(bf16[256,256]{1,0:T(8,128)(2,1)} %constant.46.clone.kron_hi) | copy-start | bytes 393220
  5.7 0.9 %copy-start.12 = (f32[3,32,256]{2,1,0:T(8,128)S(1)}, f32[3,32,256]{2,1,0:T(8,128)}, u32[]{:S(2)}) copy-start(f32[3,32,256]{2,1,0:T(8,128)} %constant.55.clone.side) | copy-start | bytes 294916
  6.6 0.7 copy-start.24
  7.2 39.0 %copy-start = (f32[2,32,32,128]{3,2,1,0:T(8,128)S(1)}, f32[2,32,32,128]{3,2,1,0:T(8,128)}, u32[]{:S(2)}) copy-start(f32[2,32,32,128]{3,2,1,0:T(8,128)} %constant.57.clone.inv) | copy-start | bytes 3145732
  7.2 39.0 %copy-start.1 = (f32[2,32,32,128]{3,2,1,0:T(8,128)S(1)}, f32[2,32,32,128]{3,2,1,0:T(8,128)}, u32[]{:S(2)}) copy-start(f32[2,32,32,128]{3,2,1,0:T(8,128)} %constant.56.clone.fwd) | copy-start | bytes 3145732
  12.3 33.9 %copy-start.16 = (f32[256,128]{1,0:T(8,128)S(1)}, f32[256,128]{1,0:T(8,128)}, u32[]{:S(2)}) copy-start(f32[256,128]{1,0:T(8,128)} %constant.59.clone.lam_d) | copy-start | bytes 393220
  12.4 33.9 %copy-start.17 = (bf16[256,128]{1,0:T(8,128)(2,1)S(1)}, bf16[256,128]{1,0:T(8,128)(2,1)}, u32[]{:S(2)}) copy-start(bf16[256,128]{1,0:T(8,128)(2,1)} %constant.53.clone.idft_lo) | copy-start | bytes 196612
  12.4 33.9 %copy-start.18 = (bf16[256,128]{1,0:T(8,128)(2,1)S(1)}, bf16[256,128]{1,0:T(8,128)(2,1)}, u32[]{:S(2)}) copy-start(bf16[256,128]{1,0:T(8,128)(2,1)} %constant.52.clone.idft_hi) | copy-start | bytes 196612
  12.4 33.9 %copy-start.19 = (bf16[128,256]{1,0:T(8,128)(2,1)S(1)}, bf16[128,256]{1,0:T(8,128)(2,1)}, u32[]{:S(2)}) copy-start(bf16[128,256]{1,0:T(8,128)(2,1)} %constant.51.clone.dft_lo) | copy-start | bytes 196612
  12.4 33.9 %copy-start.20 = (bf16[128,256]{1,0:T(8,128)(2,1)S(1)}, bf16[128,256]{1,0:T(8,128)(2,1)}, u32[]{:S(2)}) copy-start(bf16[128,256]{1,0:T(8,128)(2,1)} %constant.50.clone.dft_hi) | copy-start | bytes 196612
  12.4 33.9 %copy-start.21 = (f32[32,128]{1,0:T(8,128)S(1)}, f32[32,128]{1,0:T(8,128)}, u32[]{:S(2)}) copy-start(f32[32,128]{1,0:T(8,128)} %constant.58.clone.lam_y) | copy-start | bytes 49156
  46.3 27.5 %copy-start.5 = (bf16[512,512]{1,0:T(8,128)(2,1)S(1)}, bf16[512,512]{1,0:T(8,128)(2,1)}, u32[]{:S(2)}) copy-start(bf16[512,512]{1,0:T(8,128)(2,1)} %constant.44.clone.ix2_hi) | copy-start | bytes 1572868
  46.3 27.5 %copy-start.11 = (bf16[256,256]{1,0:T(8,128)(2,1)S(1)}, bf16[256,256]{1,0:T(8,128)(2,1)}, u32[]{:S(2)}) copy-start(bf16[256,256]{1,0:T(8,128)(2,1)} %constant.46.clone.kron_hi) | copy-start | bytes 393220
  46.4 27.5 %copy-start.13 = (f32[3,32,256]{2,1,0:T(8,128)S(1)}, f32[3,32,256]{2,1,0:T(8,128)}, u32[]{:S(2)}) copy-start(f32[3,32,256]{2,1,0:T(8,128)} %constant.55.clone.side) | copy-start | bytes 294916
  46.4 27.5 %copy-start.14 = (bf16[512,256]{1,0:T(8,128)(2,1)S(1)}, bf16[512,256]{1,0:T(8,128)(2,1)}, u32[]{:S(2)}) copy-start(bf16[512,256]{1,0:T(8,128)(2,1)} %constant.43.clone.ix_lo) | copy-start | bytes 786436
  46.4 27.5 %copy-start.15 = (bf16[512,256]{1,0:T(8,128)(2,1)S(1)}, bf16[512,256]{1,0:T(8,128)(2,1)}, u32[]{:S(2)}) copy-start(bf16[512,256]{1,0:T(8,128)(2,1)} %constant.42.clone.ix_hi) | copy-start | bytes 786436
  50.0 23.9 %copy-start.4 = (bf16[512,512]{1,0:T(8,128)(2,1)S(1)}, bf16[512,512]{1,0:T(8,128)(2,1)}, u32[]{:S(2)}) copy-start(bf16[512,512]{1,0:T(8,128)(2,1)} %constant.45.clone.ix2_lo) | copy-start | bytes 1572868
  50.0 23.9 %copy-start.7 = (f32[4,32,256]{2,1,0:T(8,128)S(1)}, f32[4,32,256]{2,1,0:T(8,128)}, u32[]{:S(2)}) copy-start(f32[4,32,256]{2,1,0:T(8,128)} %constant.54.clone.off1) | copy-start | bytes 393220
  50.0 23.9 %copy-start.9 = (bf16[256,256]{1,0:T(8,128)(2,1)S(1)}, bf16[256,256]{1,0:T(8,128)(2,1)}, u32[]{:S(2)}) copy-start(bf16[256,256]{1,0:T(8,128)(2,1)} %constant.47.clone.kron_lo) | copy-start | bytes 393220

commit v2 on v1

v2 whole, which is shorter than its diff:
```python
import functools
import math

import jax
import jax.numpy as jnp
import ml_dtypes
import numpy as np
from jax import lax
from jax.experimental import pallas as pl
from jax.experimental.pallas import tpu as pltpu
from jax.sharding import PartitionSpec as P

screening = 0.0015
NX = 1024
NY = 1024
NZ = 64
GZ = 8
GY = 32
LZ = NZ // GZ
LY = NY // GY
DEV = GZ * GY
KX = NX // DEV
SMALL = 144
SHARED = 512 + 3 * SMALL
FORWARD = SHARED + 8 * 256
BACKWARD = FORWARD + 8 * 256
SLABS = BACKWARD + 512
LEAF = GY + DEV
BOOK = LEAF + 4 * GY * LY
f32 = jnp.float32
bf16 = jnp.bfloat16


def basis(count):
    j = np.arange(count)[:, None]
    m = np.arange(count)[None, :]
    half = count // 2
    wave = np.where(m <= half, m, m - half)
    angle = 2.0 * np.pi / count * ((j * wave) % count)
    scale = np.where((m == 0) | (m == half), 1.0, math.sqrt(2.0)) / math.sqrt(count)
    return np.where(m <= half, np.cos(angle), np.sin(angle)) * scale


def eigen(count):
    m = np.arange(count)
    half = count // 2
    wave = np.where(m <= half, m, m - half)
    return 2.0 - 2.0 * np.cos(2.0 * np.pi / count * wave)


def two(x):
    hi = np.asarray(x, np.float64).astype(ml_dtypes.bfloat16)
    lo = (x - hi.astype(np.float64)).astype(ml_dtypes.bfloat16)
    return hi, lo


@functools.lru_cache(maxsize=None)
def tables():
    half = NX // 2
    tx = basis(NX)
    ex = eigen(NX)
    columns = [
        np.concatenate([np.arange(0, half + 1, 4), half + np.arange(4, half, 4)]),
        np.concatenate([np.arange(2, half, 4), half + np.arange(2, half, 4)]),
    ]
    quarter = np.arange(256)
    turn = 2.0 * np.pi / NX * (quarter[:, None] * (4 * quarter[None, :] + 1) % NX)
    waves = math.sqrt(2.0 / NX) * np.cos(turn), math.sqrt(2.0 / NX) * np.sin(turn)
    parts = [tx[:256, columns[0]], tx[:256, columns[1]], *waves]
    lam_odd = 2.0 - 2.0 * np.cos(2.0 * np.pi / NX * (4 * quarter + 1))
    lam_x = np.stack([ex[columns[0]], ex[columns[1]], lam_odd, lam_odd])

    sine = np.zeros((LY, LY))
    sine[0, 0] = 1.0
    m = np.arange(1, LY)
    sine[1:, 1:] = math.sqrt(2.0 / LY) * np.sin(np.pi * m[:, None] * m[None, :] / LY)
    mu = np.full((LY,), 2.0)
    mu[1:] = 2.0 - 2.0 * np.cos(np.pi * m / LY)
    kron = np.kron(np.eye(LZ), sine)
    q_first = sine[:, 1].copy()
    q_first[0] = 0.0
    q_last = sine[:, LY - 1].copy()
    q_last[0] = 0.0
    mask = np.ones((LY,))
    mask[0] = 0.0
    side = np.stack([np.repeat(v[:, None], 256, axis=1) for v in (q_first, q_last, mask)])
    small = np.zeros((SMALL, 256))
    small[:KX] = lam_x
    small[16 : 16 + 3 * LY] = side.reshape(3 * LY, 256)
    small[16 + 3 * LY :] = mu[:, None] + screening
    rest, thirds = small.astype(np.float32).astype(np.float64), []
    for _ in range(3):
        thirds.append(rest.astype(ml_dtypes.bfloat16))
        rest = rest - thirds[-1].astype(np.float64)
    pack = [*two(kron), *thirds]
    for part in parts:
        pack += two(part)
    for part in parts:
        pack += two(part.T)

    ty = basis(NY)
    ey = eigen(NY)
    main = basis(GY)
    partner = np.zeros((GY, GY))
    for p in range(1, GY // 2):
        partner[:, p] = main[:, GY // 2 + p]
        partner[:, GY // 2 + p] = main[:, p]
    wave = np.where(np.arange(NY) <= NY // 2, np.arange(NY), np.arange(NY) - NY // 2)
    is_cos = np.arange(NY) <= NY // 2
    fold = wave % GY
    fold = np.minimum(fold, GY - fold)
    order = np.zeros((GY, GY), np.int64)
    for p in range(GY):
        if p in (0, GY // 2):
            order[:, p] = np.nonzero(fold == p)[0]
        elif p < GY // 2:
            order[:, p] = np.nonzero((fold == p) & is_cos)[0]
        else:
            order[:, p] = np.nonzero((fold == p - GY // 2) & ~is_cos)[0]
    shaped = ty.reshape(GY, LY, NY)[:, :, order]
    a_y = np.einsum("bvjp,bp->vjp", shaped, main)
    b_y = np.einsum("bvjp,bp->vjp", shaped, partner)
    a_m = np.einsum("mv,vjp->mjp", sine, a_y)
    b_m = np.einsum("mv,vjp->mjp", sine, b_y)
    a_m = np.tile(a_m, (1, 1, KX))
    b_m = np.tile(b_m, (1, 1, KX))
    lam_y = np.tile(ey[order], (1, KX)) + screening
    lam_d = np.repeat(lam_x.T, GY, axis=1)
    spread = np.eye(KX)
    dft = np.concatenate([np.kron(spread, main), np.kron(spread, partner)], axis=1)
    pack += two(dft)
    pack.append(np.concatenate(two(dft.T), axis=1))
    pack = np.concatenate(pack, axis=0)
    assert pack.shape == (SLABS, 256)
    later = pack[FORWARD:BACKWARD]
    both = np.stack([a_m, b_m])
    book = [lam_y, lam_d, both, both.transpose(0, 2, 1, 3)]
    book = np.concatenate([part.reshape(-1, 128) for part in book], axis=0).astype(np.float32)
    assert book.shape == (BOOK, 128)
    return pack, book, later


def split(x):
    hi = x.astype(bf16)
    return hi, (x - hi.astype(f32)).astype(bf16)


def dot(a, b):
    return lax.dot_general(a, b, (((1,), (0,)), ((), ())), preferred_element_type=f32)


def dot3(a, b):
    return dot(a[0], b[0]) + (dot(a[0], b[1]) + dot(a[1], b[0]))


def wall_rows(rows, width):
    first = lax.axis_index("gz") * LZ
    inside = first + LZ < NZ
    places = [first + t for t in range(LZ)] + [jnp.minimum(first + LZ, NZ - 1)]
    heights = [jnp.concatenate([rows[pl.ds(place, 1), :]] * (width // 128), axis=1) for place in places]
    gaps = [0.5 * (heights[t] + heights[t + 1]) for t in range(LZ)]
    keep = jnp.where(inside, 1.0, 0.0).astype(f32)
    lower = [None] + [1.0 / (gaps[t - 1] * heights[t]) for t in range(1, LZ + 1)]
    upper = [1.0 / (gaps[t] * heights[t]) for t in range(LZ)]
    inverse = [1.0 / heights[t] for t in range(LZ + 1)]
    lower[LZ] = lower[LZ] * keep
    upper[LZ - 1] = upper[LZ - 1] * keep
    inverse[LZ] = inverse[LZ] * keep
    return lower, upper, inverse


def block_pivots(off, mask, lower, upper):
    pivots = [None] * LZ
    for t in range(1, LZ):
        diagonal = off + (lower[t] + upper[t])
        if t > 1:
            diagonal = diagonal - (lower[t] * upper[t - 1]) * pivots[t - 1]
        pivots[t] = mask / diagonal
    return pivots


def block_solve(right, pivots, lower, upper):
    value = [None] * LZ
    for t in range(1, LZ):
        term = right[t] if t == 1 else right[t] + lower[t] * value[t - 1]
        value[t] = term * pivots[t]
    for t in range(LZ - 2, 0, -1):
        value[t] = value[t] + upper[t] * pivots[t] * value[t + 1]
    return value


def eliminate(
    spacing_in, stream_in, span_in, wall_in, pack_in, book_in,
    message, kept, heights, book, slabs, low, up, pivot, block, shared,
    spacing, stream, span, wall, pack, part_hi, part_lo, ends, cell_sem, table_sem,
):
    first_copy = pltpu.make_async_copy(spacing_in, spacing, table_sem.at[0])
    first_copy.start()
    leaf = pltpu.make_async_copy(book_in.at[pl.ds(0, LEAF)], book.at[pl.ds(0, LEAF)], table_sem.at[4])
    leaf.start()
    copies = []
    for t in range(0, LZ, 2):
        here = pl.ds(t, 2)
        trio = [
            pltpu.make_async_copy(source.at[here], target.at[here], cell_sem.at[t // 2, k])
            for k, (source, target) in enumerate(((stream_in, stream), (span_in, span), (wall_in, wall)))
        ]
        for copy in trio:
            copy.start()
        copies.append(trio)
    table_copies = []
    moves = (
        (pack_in.at[pl.ds(0, SHARED)], shared),
        (pack_in.at[pl.ds(SHARED, 1024)], pack.at[pl.ds(0, 1024)]),
        (pack_in.at[pl.ds(SHARED + 1024, 1024)], pack.at[pl.ds(1024, 1024)]),
    )
    for k, (source, target) in enumerate(moves):
        table_copies.append(pltpu.make_async_copy(source, target, table_sem.at[k + 1]))
        table_copies[-1].start()
    ahead = [
        pltpu.make_async_copy(pack_in.at[pl.ds(BACKWARD, 512)], slabs, table_sem.at[5]),
        pltpu.make_async_copy(
            book_in.at[pl.ds(LEAF, BOOK - LEAF)], book.at[pl.ds(LEAF, BOOK - LEAF)], table_sem.at[6]
        ),
    ]
    for copy in ahead:
        copy.start()
    first_copy.wait()
    for z in range(NZ):
        heights[z : z + 1, :] = jnp.full((1, 128), spacing[z], f32)
    tall = heights[...]
    layer = lax.broadcasted_iota(jnp.int32, (NZ, 128), 0)
    gap = 0.5 * (tall + pltpu.roll(tall, NZ - 1, axis=0))
    low[...] = jnp.where(layer == 0, 0.0, 1.0 / (pltpu.roll(gap, 1, axis=0) * tall))
    up[...] = jnp.where(layer == NZ - 1, 0.0, 1.0 / (gap * tall))
    leaf.wait()
    me = lax.axis_index("gy") * GZ + lax.axis_index("gz")
    off = book[pl.ds(0, GY), :] + book[pl.ds(GY + me, 1), :]
    half = NZ // 2
    last = [None, None]

    def wall_step(s):
        for side, z in enumerate((s, NZ - 1 - s)):
            diagonal = off + (low[z : z + 1, :] + up[z : z + 1, :])
            if s > 0 and side == 0:
                diagonal = diagonal - (low[z : z + 1, :] * up[z - 1 : z, :]) * last[0]
            if s > 0 and side == 1:
                diagonal = diagonal - (up[z : z + 1, :] * low[z + 1 : z + 2, :]) * last[1]
            last[side] = 1.0 / diagonal
            pivot[z] = last[side]

    lower, upper, inverse = wall_rows(heights, NX)
    rows = lax.broadcasted_iota(jnp.int32, (LY, NX), 0)
    for t in range(LZ + 2):
        if t < LZ:
            if t % 2 == 0:
                for copy in copies[t // 2]:
                    copy.wait()
            u = stream[t]
            v = span[t]
            w = wall[t]
            shifted = jnp.where(rows == 0, 0.0, pltpu.roll(v, 1, axis=0))
            d = (pltpu.roll(u, 1, axis=1) - u) + (shifted - v)
            d = d - w * inverse[t] if t == 0 else d + (wall[t - 1] - w) * inverse[t]
        elif t == LZ:
            d = wall[LZ - 1] * inverse[LZ]
        else:
            d = jnp.concatenate([span[z, LY - 1 :, :] for z in range(LZ)] + [jnp.zeros((8, NX), f32)], axis=0)
        even = d[:, :512] + d[:, 512:]
        odd = d[:, :512] - d[:, 512:]
        here = pl.ds(t * LY, d.shape[0])
        pieces = (even[:, :256] + even[:, 256:], even[:, :256] - even[:, 256:], odd[:, :256], odd[:, 256:], -odd[:, 256:])
        for k, piece in enumerate(pieces):
            hi, lo = split(piece)
            part_hi[here, 256 * k : 256 * (k + 1)] = hi
            part_lo[here, 256 * k : 256 * (k + 1)] = lo
        if t < LZ:
            for step in range(half * t // LZ, half * (t + 1) // LZ):
                wall_step(step)
    table_copies[0].wait()
    lower, upper, inverse = wall_rows(heights, 256)
    small = sum(shared[512 + k * SMALL : 512 + (k + 1) * SMALL, :].astype(f32) for k in range(3))
    q_first, q_last, mask, mu = (small[16 + k * LY : 16 + (k + 1) * LY] for k in range(4))

    def transform(piece, wave):
        a = (part_hi[:, 256 * piece : 256 * (piece + 1)], part_lo[:, 256 * piece : 256 * (piece + 1)])
        first = 512 * wave
        return dot3(a, (pack[first : first + 256, :], pack[first + 256 : first + 512, :]))

    for i in range(KX):
        if i < 2:
            table_copies[1].wait() if i == 0 else None
            lines = transform(i, i)
        elif i == 2:
            table_copies[2].wait()
            lines = transform(2, 2) + transform(4, 3)
        else:
            lines = transform(2, 3) + transform(3, 2)
        cells = dot3((shared[:256, :], shared[256:512, :]), split(lines[: LZ * LY]))
        crown = dot3((shared[:LY, :LY], shared[256 : 256 + LY, :LY]), split(lines[LZ * LY : (LZ + 1) * LY]))
        edge = lines[(LZ + 1) * LY : (LZ + 1) * LY + LZ]
        kept[i] = cells
        layers = [cells[t * LY : (t + 1) * LY] for t in range(LZ)]
        pivots = block_pivots(mu + small[i : i + 1], mask, lower, upper)
        for t in range(1, LZ):
            block[i, (t - 1) * LY : t * LY, :] = pivots[t]
        inner = block_solve(layers, pivots, lower, upper)
        ends[i * LY : (i + 1) * LY, :] = layers[0] + upper[0] * inner[1]
        ends[128 + i * LY : 128 + (i + 1) * LY, :] = crown + lower[LZ] * inner[LZ - 1]
        own = [jnp.zeros((1, 256), f32)]
        following = [jnp.zeros((1, 256), f32)]
        for t in range(1, LZ):
            own.append(layers[t][:1] + jnp.sum(inner[t] * q_first, axis=0, keepdims=True))
            following.append(jnp.sum(inner[t] * q_last, axis=0, keepdims=True))
        ends[256 + i * LZ : 256 + (i + 1) * LZ, :] = jnp.concatenate(own, axis=0)
        ends[320 + i * LZ : 320 + (i + 1) * LZ, :] = edge + jnp.concatenate(following, axis=0)
    ends[256 + KX * LZ : 320, :] = jnp.zeros((64 - KX * LZ, 256), f32)
    ends[320 + KX * LZ : 384, :] = jnp.zeros((64 - KX * LZ, 256), f32)
    for r in range(3):
        message[pl.ds(r, DEV, stride=3), :] = ends[128 * r : 128 * (r + 1), :].T
    for copy in ahead:
        copy.wait()


def interface(
    arrived, book, slabs, low, up, pivot, reply, value, spec, lines, top, back,
):
    dft_hi, dft_lo, idft = slabs[:128, :], slabs[128:256, :], slabs[256:, :]
    idft_hi, idft_lo = idft[:, :128], idft[:, 128:]
    fwd = lambda k, m: book[pl.ds(LEAF + (k * LY + m) * GY, GY), :]
    inv = lambda k, j: book[pl.ds(LEAF + 2 * LY * GY + (k * GY + j) * LY, LY), :]
    half = NZ // 2
    lane = lax.broadcasted_iota(jnp.int32, (GY, 128), 1)
    field = [arrived[pl.ds(3 * a, GY, stride=3 * GZ), :] for a in range(GZ)]
    for a in range(1, GZ):
        field[a] = field[a] + arrived[pl.ds(3 * (a - 1) + 1, GY, stride=3 * GZ), :]
    for g in range(2):
        blocks = []
        for i in range(KX):
            block = None
            for k in range(4):
                moved = pltpu.roll(field[4 * g + k], (32 * (k - i)) % 128, axis=1)
                block = moved if block is None else jnp.where(lane // 32 == k, moved, block)
            blocks.append(block)
        stacked = jnp.concatenate(blocks, axis=0).T
        spec[128 * g : 128 * (g + 1), :] = dot3(split(stacked), (dft_hi, dft_lo))
    sides = []
    for a in range(GZ):
        rest = arrived[pl.ds(3 * a + 2, GY, stride=3 * GZ), :]
        sides.append(rest + pltpu.roll(pltpu.roll(rest, 64, axis=1), 1, axis=0))
    blocks = []
    for i in range(KX):
        block = jnp.zeros((GY, 128), f32)
        for a in range(GZ):
            moved = pltpu.roll(sides[a], (8 * (a - i)) % 128, axis=1)
            block = jnp.where(lane // 8 == a, moved, block)
        blocks.append(block)
    stacked = jnp.concatenate(blocks, axis=0).T[:NZ]
    lines[...] = dot3(split(stacked), (dft_hi[:, :128], dft_lo[:, :128]))
    for g in range(2):
        total = [jnp.zeros((GY, 128), f32)] * 4
        for m in range(LY):
            c_main = fwd(0, m)
            c_partner = fwd(1, m)
            for k in range(4):
                row = 128 * g + 32 * k + m
                total[k] = total[k] + c_main * spec[row : row + 1, :128] + c_partner * spec[row : row + 1, 128:]
        for k in range(4):
            top[4 * g + k] = total[k]
    weight = fwd(0, 0)
    for s in range(half):
        for z in (s, NZ - 1 - s):
            right = weight * lines[z : z + 1, :]
            if z % LZ == 0:
                right = right + top[z // LZ]
            if s > 0:
                if z < half:
                    right = right + low[z : z + 1, :] * value[z - 1]
                else:
                    right = right + up[z : z + 1, :] * value[z + 1]
            value[z] = right * pivot[z]
    alpha = up[half - 1 : half, :] * pivot[half - 1]
    beta = low[half : half + 1, :] * pivot[half]
    below = (value[half - 1] + alpha * value[half]) / (1.0 - alpha * beta)
    above = value[half] + beta * below
    for s in range(half):
        for z in (half - 1 - s, half + s):
            if z < half:
                if s > 0:
                    below = value[z] + up[z : z + 1, :] * pivot[z] * below
                now = below
            else:
                if s > 0:
                    above = value[z] + low[z : z + 1, :] * pivot[z] * above
                now = above
            lines[z : z + 1, :] = jnp.sum(now * weight, axis=0, keepdims=True)
            if z % LZ == 0:
                top[z // LZ] = now
    for g in range(2):
        total = [jnp.zeros((LY, 128), f32)] * 4
        other = [jnp.zeros((LY, 128), f32)] * 4
        for j in range(GY):
            c_main = inv(0, j)
            c_partner = inv(1, j)
            for k in range(4):
                row = top[4 * g + k, j : j + 1, :]
                total[k] = total[k] + c_main * row
                other[k] = other[k] + c_partner * row
        for k in range(4):
            spec[128 * g + 32 * k : 128 * g + 32 * (k + 1), :128] = total[k]
            spec[128 * g + 32 * k : 128 * g + 32 * (k + 1), 128:] = other[k]
    for g in range(2):
        back[...] = dot3(split(spec[128 * g : 128 * (g + 1), :]), (idft_hi, idft_lo)).T
        for k in range(4):
            block = None
            for i in range(KX):
                moved = pltpu.roll(back[32 * i : 32 * (i + 1), :], (32 * (i - k)) % 128, axis=1)
                block = moved if block is None else jnp.where(lane // 32 == i, moved, block)
            a = 4 * g + k
            reply[pl.ds(3 * a, GY, stride=3 * GZ), :] = block
            if a > 0:
                reply[pl.ds(3 * (a - 1) + 1, GY, stride=3 * GZ), :] = block
    reply[pl.ds(3 * (GZ - 1) + 1, GY, stride=3 * GZ), :] = jnp.zeros((GY, 128), f32)
    rest = dot3(split(lines[...]), (idft_hi[:128, :], idft_lo[:128, :]))
    back[...] = jnp.concatenate([rest, rest], axis=0).T
    pieces = []
    for i in range(KX):
        piece = back[32 * i : 32 * (i + 1), :]
        pieces.append(jnp.where(lane < 64, piece, pltpu.roll(piece, GY - 1, axis=0)))
    for a in range(GZ):
        block = jnp.zeros((GY, 128), f32)
        for i in range(KX):
            moved = pltpu.roll(pieces[i], (8 * (i - a)) % 128, axis=1)
            block = jnp.where((lane % 64) // 8 == i, moved, block)
        reply[pl.ds(3 * a + 2, GY, stride=3 * GZ), :] = block


def restore(
    rows, arrived, kept, shared, block, pack, pressure, ends, result, out_sem,
):
    lower, upper, _ = wall_rows(rows, 256)
    small = sum(shared[512 + k * SMALL : 512 + (k + 1) * SMALL, :].astype(f32) for k in range(3))
    q_first, q_last, mask = (small[16 + k * LY : 16 + (k + 1) * LY] for k in range(3))
    for r in range(3):
        ends[128 * r : 128 * (r + 1), :] = arrived[pl.ds(r, DEV, stride=3), :].T
    lines = []
    for i in range(KX):
        floor = ends[i * LY : (i + 1) * LY, :]
        ceiling = ends[128 + i * LY : 128 + (i + 1) * LY, :]
        pivots = [None] + [block[i, (t - 1) * LY : t * LY, :] for t in range(1, LZ)]
        right = [None] * LZ
        near = [None] * LZ
        for t in range(1, LZ):
            near[t] = ends[256 + i * LZ + t : 256 + i * LZ + t + 1, :]
            far = ends[320 + i * LZ + t : 320 + i * LZ + t + 1, :]
            right[t] = kept[i, t * LY : (t + 1) * LY, :] + (q_first * near[t] + q_last * far)
        right[1] = right[1] + lower[1] * floor
        right[LZ - 1] = right[LZ - 1] + upper[LZ - 1] * ceiling
        inner = block_solve(right, pivots, lower, upper)
        layers = [floor] + [inner[t] + (1.0 - mask) * near[t] for t in range(1, LZ)]
        modes = jnp.concatenate(layers, axis=0)
        lines.append(dot3((shared[:256, :], shared[256:512, :]), split(modes)))

    def transform(line, wave):
        first = 512 * wave
        return dot3(line, (pack[first : first + 256, :], pack[first + 256 : first + 512, :]))

    minus = split(-lines[2])
    lines = [split(line) for line in lines]
    even = transform(lines[0], 0)
    odd = transform(lines[1], 1)
    copies = []
    for q in range(2):
        if q == 0:
            whole = even + odd
            swing = transform(lines[2], 2) + transform(lines[3], 3)
        else:
            whole = even - odd
            swing = transform(minus, 3) + transform(lines[3], 2)
        for k, piece in ((q, whole + swing), (q + 2, whole - swing)):
            here = pl.ds(256 * k, 256)
            result[:, :, 256 * k : 256 * (k + 1)] = piece.reshape(LZ, LY, 256)
            copy = pltpu.make_async_copy(result.at[:, :, here], pressure.at[:, :, here], out_sem.at[k])
            copy.start()
            copies.append(copy)
    for copy in copies:
        copy.wait()


def on_device(streamwise, spanwise, wall_normal, spacing):
    far = lambda x: pltpu.with_memory_space_constraint(x, pltpu.HBM)
    near = lambda x: pltpu.with_memory_space_constraint(x, pltpu.VMEM)
    pack, book, later = (jnp.asarray(part) for part in tables())
    pack, book = far(pack), far(book)
    vmem = pl.BlockSpec(memory_space=pltpu.VMEM)
    hbm = pl.BlockSpec(memory_space=pltpu.HBM)
    params = pltpu.CompilerParams(vmem_limit_bytes=50 * 2**20)
    shape = jax.ShapeDtypeStruct
    message, kept, heights, book, slabs, low, up, pivot, block, shared = pl.pallas_call(
        eliminate,
        out_shape=(
            pltpu.VMEM((3 * DEV, 128), f32),
            pltpu.VMEM((KX, LZ * LY, 256), f32),
            pltpu.VMEM((NZ, 128), f32),
            pltpu.VMEM((BOOK, 128), f32),
            pltpu.VMEM((512, 256), bf16),
            pltpu.VMEM((NZ, 128), f32),
            pltpu.VMEM((NZ, 128), f32),
            pltpu.VMEM((NZ, GY, 128), f32),
            pltpu.VMEM((KX, (LZ - 1) * LY, 256), f32),
            pltpu.VMEM((SHARED, 256), bf16),
        ),
        in_specs=[hbm] * 6,
        out_specs=(vmem,) * 10,
        scratch_shapes=[
            pltpu.SMEM((NZ,), f32),
            pltpu.VMEM((LZ, LY, NX), f32),
            pltpu.VMEM((LZ, LY, NX), f32),
            pltpu.VMEM((LZ, LY, NX), f32),
            pltpu.VMEM((8 * 256, 256), bf16),
            pltpu.VMEM(((LZ + 1) * LY + 16, NX + 256), bf16),
            pltpu.VMEM(((LZ + 1) * LY + 16, NX + 256), bf16),
            pltpu.VMEM((384, 256), f32),
            pltpu.SemaphoreType.DMA((LZ // 2, 3)),
            pltpu.SemaphoreType.DMA((7,)),
        ],
        compiler_params=params,
        name="eliminate",
    )(far(spacing), far(streamwise), far(spanwise), far(wall_normal), pack, book)
    axes = ("gy", "gz")
    trade = lambda x: lax.all_to_all(
        x.reshape(DEV, 1, 384), axes, split_axis=0, concat_axis=0, tiled=True
    ).reshape(3 * DEV, 128)
    arrived = trade(message)
    reply = pl.pallas_call(
        interface,
        out_shape=pltpu.VMEM((3 * DEV, 128), f32),
        in_specs=[vmem] * 6,
        out_specs=vmem,
        scratch_shapes=[
            pltpu.VMEM((NZ, GY, 128), f32),
            pltpu.VMEM((256, 256), f32),
            pltpu.VMEM((NZ, 128), f32),
            pltpu.VMEM((GZ, GY, 128), f32),
            pltpu.VMEM((128, 128), f32),
        ],
        compiler_params=params,
        name="interface",
    )(near(arrived), near(book), near(slabs), near(low), near(up), near(pivot))
    answered = trade(reply)
    return pl.pallas_call(
        restore,
        out_shape=shape((LZ, LY, NX), f32),
        in_specs=[vmem] * 6,
        out_specs=hbm,
        scratch_shapes=[
            pltpu.VMEM((384, 256), f32),
            pltpu.VMEM((LZ, LY, NX), f32),
            pltpu.SemaphoreType.DMA((4,)),
        ],
        compiler_params=params,
        name="restore",
    )(near(heights), near(answered), near(kept), near(shared), near(block), near(later))


def solution(mesh):
    placed = (P("gz", "gy", None), P("gz", "gy", None), P("gz", "gy", None), P())
    return jax.shard_map(
        on_device, mesh=mesh, in_specs=placed, out_specs=P("gz", "gy", None), check_vma=False
    )
```

time: 78 us -> 68.5 us (0.88)
  local copies, waits for them, and re-layouts: 7.34 us -> 0.01 us
  Pallas kernels: 12.4 us -> 11.5 us
  blocking collectives: 57.6 us -> 56.8 us
    unnamed x50 -> x2, local copies, waits for them, and re-layouts: 7.34 us -> 0.01 us
    pallas_call x3, Pallas kernels: 12.4 us -> 11.5 us  [the longest x1 5.99 us: on_device(): pl.pallas_call(eliminate, out_shape=(pltpu.VMEM((3 * DEV, 128), f32), plt...]
    all_to_all x2, blocking collectives: 57.6 us -> 56.8 us  [on_device(): lax.all_to_all(x.reshape(DEV, 1, 384), axes, split_axis=0, concat_axis=0,...]
where the time goes in v2:
time: 68.5 us; the launch traced here: 68.3 us
  blocking collectives  56.8 us (83%)
  Pallas kernels  11.5 us (17%)
    all_to_all x2, blocking collectives, on_device(): lax.all_to_all(x.reshape(DEV, 1, 384), axes, split_axis=0, concat_axis=0,...  56.8 us
    pallas_call x1, Pallas kernels, on_device(): pl.pallas_call(eliminate, out_shape=(pltpu.VMEM((3 * DEV, 128), f32), plt...  5.99 us
    pallas_call x1, Pallas kernels, on_device(): pl.pallas_call(interface, out_shape=pltpu.VMEM((3 * DEV, 128), f32), in_s...  2.96 us
    pallas_call x1, Pallas kernels, on_device(): pl.pallas_call(restore, out_shape=shape((LZ, LY, NX), f32), in_specs=[vme...  2.56 us

profile of v2, /device:TPU:1, one launch (start us, length us, event | category | flops | bytes accessed | tf_op | source)
XLA Modules:
  0.0 68.3 jit_solution(3148936273802394439)
XLA Ops:
  0.0 6.0 %eliminate.1 = (f32[768,128]{1,0:T(8,128)S(1)}, f32[4,256,256]{2,1,0:T(8,128)S(1)}, f32[64,128]{1,0:T(8,128)S(1)}, f32[4384,128]{1,0:T(8,128)S(1)}, bf16[512,256...) custom-call(f32[64]{0:T(128)} %spacing_in.1, ...), custom_call_target="tpu_custom_call" | custom-call | tf_op jit(solution)/shard_map/eliminate/pallas_call | solution.py:499
  6.0 33.6 %all_to_all.10 = f32[256,1,384]{2,1,0:T(1,128)S(1)} all-to-all(f32[256,1,384]{2,1,0:T(1,128)S(1)} %bitcast.7), channel_id=1, replica_groups=mesh['gz'=8,'gy'=32] {'gy','gz'}, dimensions={0} | all-to-all | bytes 786432 | tf_op jit(solution)/shard_map/all_to_all | solution.py:531
  39.6 0.0 copy-start
  39.6 3.0 %interface.1 = f32[768,128]{1,0:T(8,128)S(1)} custom-call(f32[768,128]{1,0:T(8,128)S(1)} %bitcast.5, f32[4384,128]{1,0:T(8,128)S(1)} %get-tuple-element.17.book, bf16[512,256]{1,0:T(8,128)(2,1)S(1)} %get-tuple-element.18.slabs, f32[64,128]{1,0:T(8,128)S(1)} %get-tuple-element.19.low, f32[64,128]{1,0:T(8,128)S(1)} %get-tuple-element.20.up, ...), custom_call_target="tpu_custom_call" | custom-call | tf_op jit(solution)/shard_map/interface/pallas_call | solution.py:535
  42.6 23.2 %all_to_all.11 = f32[256,1,384]{2,1,0:T(1,128)S(1)} all-to-all(f32[256,1,384]{2,1,0:T(1,128)S(1)} %bitcast.6), channel_id=1, replica_groups=mesh['gz'=8,'gy'=32] {'gy','gz'}, dimensions={0} | all-to-all | bytes 786432 | tf_op jit(solution)/shard_map/all_to_all | solution.py:531
  65.8 0.0 copy-done
  65.8 2.6 %restore.1 = f32[8,32,1024]{2,1,0:T(8,128)} custom-call(f32[64,128]{1,0:T(8,128)S(1)} %get-tuple-element.15.rows, f32[768,128]{1,0:T(8,128)S(1)} %bitcast.4, f32[4,256,256]{2,1,0:T(8,128)S(1)} %get-tuple-element.22.kept, bf16[944,256]{1,0:T(8,128)(2,1)S(1)} %get-tuple-element.23.shared, f32[4,224,256]{2,1,0:T(8,128)S(1)} %get-tuple-element.24.block, ...), custom_call_target="tpu_custom_call" | custom-call | tf_op jit(solution)/shard_map/restore/pallas_call | solution.py:551
Async XLA Ops:
  39.6 26.2 %copy-start = (bf16[2048,256]{1,0:T(8,128)(2,1)S(1)}, bf16[2048,256]{1,0:T(8,128)(2,1)}, u32[]{:S(2)}) copy-start(bf16[2048,256]{1,0:T(8,128)(2,1)} %constant.8.clone.pack) | copy-start | bytes 3145732

commit v3 on v2

--- a/solution.py
+++ b/solution.py
@@ -26,6 +26,9 @@
 BACKWARD = FORWARD + 8 * 256
 SLABS = BACKWARD + 512
 LEAF = GY + DEV
+EARLY = 6
+HALF = EARLY * LY
+ROWS = (HALF, (LZ + 1) * LY - HALF + 16)
 BOOK = LEAF + 4 * GY * LY
 f32 = jnp.float32
 bf16 = jnp.bfloat16
@@ -153,6 +156,18 @@
     return dot(a[0], b[0]) + (dot(a[0], b[1]) + dot(a[1], b[0]))
 
 
+def stacked3(a, count, high, low):
+    full = dot(a, high)
+    return full[:count] + (full[count:] + dot(a[:count], low))
+
+
+def sandwich(kron, lines):
+    hi, lo = split(lines)
+    full = dot(kron, hi)
+    count = lines.shape[0]
+    return full[:count] + (full[count:] + dot(kron[:count], lo))
+
+
 def wall_rows(rows, width):
     first = lax.axis_index("gz") * LZ
     inside = first + LZ < NZ
@@ -192,7 +207,7 @@
 def eliminate(
     spacing_in, stream_in, span_in, wall_in, pack_in, book_in,
     message, kept, heights, book, slabs, low, up, pivot, block, shared,
-    spacing, stream, span, wall, pack, part_hi, part_lo, ends, cell_sem, table_sem,
+    spacing, stream, span, wall, pack, part_0, part_1, part_2, part_3, part_4, part_5, ends, cell_sem, table_sem,
 ):
     first_copy = pltpu.make_async_copy(spacing_in, spacing, table_sem.at[0])
     first_copy.start()
@@ -208,15 +223,16 @@
         for copy in trio:
             copy.start()
         copies.append(trio)
-    table_copies = []
-    moves = (
-        (pack_in.at[pl.ds(0, SHARED)], shared),
-        (pack_in.at[pl.ds(SHARED, 1024)], pack.at[pl.ds(0, 1024)]),
-        (pack_in.at[pl.ds(SHARED + 1024, 1024)], pack.at[pl.ds(1024, 1024)]),
-    )
-    for k, (source, target) in enumerate(moves):
-        table_copies.append(pltpu.make_async_copy(source, target, table_sem.at[k + 1]))
-        table_copies[-1].start()
+        if t == 2:
+            table_copies = []
+            moves = (
+                (pack_in.at[pl.ds(0, SHARED)], shared),
+                (pack_in.at[pl.ds(SHARED, 1024)], pack.at[pl.ds(0, 1024)]),
+                (pack_in.at[pl.ds(SHARED + 1024, 1024)], pack.at[pl.ds(1024, 1024)]),
+            )
+            for k, (source, target) in enumerate(moves):
+                table_copies.append(pltpu.make_async_copy(source, target, table_sem.at[k + 1]))
+                table_copies[-1].start()
     ahead = [
         pltpu.make_async_copy(pack_in.at[pl.ds(BACKWARD, 512)], slabs, table_sem.at[5]),
         pltpu.make_async_copy(
@@ -251,6 +267,25 @@
 
     lower, upper, inverse = wall_rows(heights, NX)
     rows = lax.broadcasted_iota(jnp.int32, (LY, NX), 0)
+    extra = []
+
+    def transform(part, wave):
+        first = 512 * wave
+        return stacked3(part[...], part.shape[0] // 2, pack[first : first + 256, :], pack[first + 256 : first + 512, :])
+
+    def transform_group(parts, group):
+        count = ROWS[group]
+        lines = [transform(parts[0], 0), transform(parts[1], 1)]
+        cosine, sine = transform(parts[2], 2), transform(parts[2], 3)
+        lines += [cosine[:count] - sine[count:], sine[:count] + cosine[count:]]
+        size = (HALF, LZ * LY - HALF)[group]
+        sines = shared[:size, :size], shared[256 : 256 + size, :size]
+        for i in range(KX):
+            kept[i, group * HALF : group * HALF + size, :] = dot3(sines, split(lines[i][:size]))
+            if group == 1:
+                crown = dot3((sines[0][:LY, :LY], sines[1][:LY, :LY]), split(lines[i][size : size + LY]))
+                extra.append((crown, lines[i][size + LY : size + LY + LZ]))
+
     for t in range(LZ + 2):
         if t < LZ:
             if t % 2 == 0:
@@ -268,38 +303,29 @@
             d = jnp.concatenate([span[z, LY - 1 :, :] for z in range(LZ)] + [jnp.zeros((8, NX), f32)], axis=0)
         even = d[:, :512] + d[:, 512:]
         odd = d[:, :512] - d[:, 512:]
-        here = pl.ds(t * LY, d.shape[0])
-        pieces = (even[:, :256] + even[:, 256:], even[:, :256] - even[:, 256:], odd[:, :256], odd[:, 256:], -odd[:, 256:])
+        pieces = (even[:, :256] + even[:, 256:], even[:, :256] - even[:, 256:], odd[:, :256], odd[:, 256:])
         for k, piece in enumerate(pieces):
             hi, lo = split(piece)
-            part_hi[here, 256 * k : 256 * (k + 1)] = hi
-            part_lo[here, 256 * k : 256 * (k + 1)] = lo
+            group = 0 if t < EARLY else 1
+            count = ROWS[group]
+            parts = ((part_0, part_1, part_2, part_2), (part_3, part_4, part_5, part_5))[group]
+            for part, level in ((hi, 0), (lo, 1)):
+                first = (level, level, 2 * level, 2 * level + 1)[k] * count + t * LY - group * HALF
+                parts[k][first : first + d.shape[0], :] = part
         if t < LZ:
             for step in range(half * t // LZ, half * (t + 1) // LZ):
                 wall_step(step)
-    table_copies[0].wait()
+        if t == EARLY - 1:
+            for copy in table_copies:
+                copy.wait()
+            transform_group((part_0, part_1, part_2), 0)
+    transform_group((part_3, part_4, part_5), 1)
     lower, upper, inverse = wall_rows(heights, 256)
     small = sum(shared[512 + k * SMALL : 512 + (k + 1) * SMALL, :].astype(f32) for k in range(3))
     q_first, q_last, mask, mu = (small[16 + k * LY : 16 + (k + 1) * LY] for k in range(4))
-
-    def transform(piece, wave):
-        a = (part_hi[:, 256 * piece : 256 * (piece + 1)], part_lo[:, 256 * piece : 256 * (piece + 1)])
-        first = 512 * wave
-        return dot3(a, (pack[first : first + 256, :], pack[first + 256 : first + 512, :]))
-
     for i in range(KX):
-        if i < 2:
-            table_copies[1].wait() if i == 0 else None
-            lines = transform(i, i)
-        elif i == 2:
-            table_copies[2].wait()
-            lines = transform(2, 2) + transform(4, 3)
-        else:
-            lines = transform(2, 3) + transform(3, 2)
-        cells = dot3((shared[:256, :], shared[256:512, :]), split(lines[: LZ * LY]))
-        crown = dot3((shared[:LY, :LY], shared[256 : 256 + LY, :LY]), split(lines[LZ * LY : (LZ + 1) * LY]))
-        edge = lines[(LZ + 1) * LY : (LZ + 1) * LY + LZ]
-        kept[i] = cells
+        cells = kept[i]
+        crown, edge = extra[i]
         layers = [cells[t * LY : (t + 1) * LY] for t in range(LZ)]
         pivots = block_pivots(mu + small[i : i + 1], mask, lower, upper)
         for t in range(1, LZ):
@@ -459,7 +485,7 @@
         inner = block_solve(right, pivots, lower, upper)
         layers = [floor] + [inner[t] + (1.0 - mask) * near[t] for t in range(1, LZ)]
         modes = jnp.concatenate(layers, axis=0)
-        lines.append(dot3((shared[:256, :], shared[256:512, :]), split(modes)))
+        lines.append(sandwich(shared[:512, :], modes))
 
     def transform(line, wave):
         first = 512 * wave
@@ -518,8 +544,12 @@
             pltpu.VMEM((LZ, LY, NX), f32),
             pltpu.VMEM((LZ, LY, NX), f32),
             pltpu.VMEM((8 * 256, 256), bf16),
-            pltpu.VMEM(((LZ + 1) * LY + 16, NX + 256), bf16),
-            pltpu.VMEM(((LZ + 1) * LY + 16, NX + 256), bf16),
+            pltpu.VMEM((2 * ROWS[0], 256), bf16),
+            pltpu.VMEM((2 * ROWS[0], 256), bf16),
+            pltpu.VMEM((4 * ROWS[0], 256), bf16),
+            pltpu.VMEM((2 * ROWS[1], 256), bf16),
+            pltpu.VMEM((2 * ROWS[1], 256), bf16),
+            pltpu.VMEM((4 * ROWS[1], 256), bf16),
             pltpu.VMEM((384, 256), f32),
             pltpu.SemaphoreType.DMA((LZ // 2, 3)),
             pltpu.SemaphoreType.DMA((7,)),

time: 68.5 us -> 67.4 us (0.984)
  Pallas kernels: 11.5 us -> 10.4 us
    pallas_call x1, Pallas kernels: 5.99 us -> 4.9 us  [on_device(): pl.pallas_call(eliminate, out_shape=(pltpu.VMEM((3 * DEV, 128), f32), plt...]
where the time goes in v3:
time: 67.4 us; the launch traced here: 67.2 us
  blocking collectives  56.8 us (84%)
  Pallas kernels  10.4 us (15%)
    all_to_all x2, blocking collectives, on_device(): lax.all_to_all(x.reshape(DEV, 1, 384), axes, split_axis=0, concat_axis=0,...  56.8 us
    pallas_call x1, Pallas kernels, on_device(): pl.pallas_call(eliminate, out_shape=(pltpu.VMEM((3 * DEV, 128), f32), plt...  4.9 us
    pallas_call x1, Pallas kernels, on_device(): pl.pallas_call(interface, out_shape=pltpu.VMEM((3 * DEV, 128), f32), in_s...  2.96 us
    pallas_call x1, Pallas kernels, on_device(): pl.pallas_call(restore, out_shape=shape((LZ, LY, NX), f32), in_specs=[vme...  2.55 us

profile of v3, /device:TPU:1, one launch (start us, length us, event | category | flops | bytes accessed | tf_op | source)
XLA Modules:
  0.0 67.2 jit_solution(8662888051228983330)
XLA Ops:
  0.0 4.9 %eliminate.1 = (f32[768,128]{1,0:T(8,128)S(1)}, f32[4,256,256]{2,1,0:T(8,128)S(1)}, f32[64,128]{1,0:T(8,128)S(1)}, f32[4384,128]{1,0:T(8,128)S(1)}, bf16[512,256...) custom-call(f32[64]{0:T(128)} %spacing_in.1, ...), custom_call_target="tpu_custom_call" | custom-call | tf_op jit(solution)/shard_map/eliminate/pallas_call | solution.py:525
  4.9 33.6 %all_to_all.10 = f32[256,1,384]{2,1,0:T(1,128)S(1)} all-to-all(f32[256,1,384]{2,1,0:T(1,128)S(1)} %bitcast.7), channel_id=1, replica_groups=mesh['gz'=8,'gy'=32] {'gy','gz'}, dimensions={0} | all-to-all | bytes 786432 | tf_op jit(solution)/shard_map/all_to_all | solution.py:561
  38.5 0.0 copy-start
  38.5 3.0 %interface.1 = f32[768,128]{1,0:T(8,128)S(1)} custom-call(f32[768,128]{1,0:T(8,128)S(1)} %bitcast.5, f32[4384,128]{1,0:T(8,128)S(1)} %get-tuple-element.17.book, bf16[512,256]{1,0:T(8,128)(2,1)S(1)} %get-tuple-element.18.slabs, f32[64,128]{1,0:T(8,128)S(1)} %get-tuple-element.19.low, f32[64,128]{1,0:T(8,128)S(1)} %get-tuple-element.20.up, ...), custom_call_target="tpu_custom_call" | custom-call | tf_op jit(solution)/shard_map/interface/pallas_call | solution.py:565
  41.5 23.2 %all_to_all.11 = f32[256,1,384]{2,1,0:T(1,128)S(1)} all-to-all(f32[256,1,384]{2,1,0:T(1,128)S(1)} %bitcast.6), channel_id=1, replica_groups=mesh['gz'=8,'gy'=32] {'gy','gz'}, dimensions={0} | all-to-all | bytes 786432 | tf_op jit(solution)/shard_map/all_to_all | solution.py:561
  64.7 0.0 copy-done
  64.7 2.5 %restore.1 = f32[8,32,1024]{2,1,0:T(8,128)} custom-call(f32[64,128]{1,0:T(8,128)S(1)} %get-tuple-element.15.rows, f32[768,128]{1,0:T(8,128)S(1)} %bitcast.4, f32[4,256,256]{2,1,0:T(8,128)S(1)} %get-tuple-element.22.kept, bf16[944,256]{1,0:T(8,128)(2,1)S(1)} %get-tuple-element.23.shared, f32[4,224,256]{2,1,0:T(8,128)S(1)} %get-tuple-element.24.block, ...), custom_call_target="tpu_custom_call" | custom-call | tf_op jit(solution)/shard_map/restore/pallas_call | solution.py:581
Async XLA Ops:
  38.5 26.2 %copy-start = (bf16[2048,256]{1,0:T(8,128)(2,1)S(1)}, bf16[2048,256]{1,0:T(8,128)(2,1)}, u32[]{:S(2)}) copy-start(bf16[2048,256]{1,0:T(8,128)(2,1)} %constant.8.clone.pack) | copy-start | bytes 3145732

commit v4 on v3

--- a/solution.py
+++ b/solution.py
@@ -206,7 +206,7 @@
 
 def eliminate(
     spacing_in, stream_in, span_in, wall_in, pack_in, book_in,
-    message, kept, heights, book, slabs, low, up, pivot, block, shared,
+    message, kept, heights, book, slabs, low, up, pivot, block, shared, lead, gain,
     spacing, stream, span, wall, pack, part_0, part_1, part_2, part_3, part_4, part_5, ends, cell_sem, table_sem,
 ):
     first_copy = pltpu.make_async_copy(spacing_in, spacing, table_sem.at[0])
@@ -264,6 +264,8 @@
                 diagonal = diagonal - (up[z : z + 1, :] * low[z + 1 : z + 2, :]) * last[1]
             last[side] = 1.0 / diagonal
             pivot[z] = last[side]
+            lead[z] = (low, up)[side][z : z + 1, :] * last[side]
+            gain[z] = (up, low)[side][z : z + 1, :] * last[side]
 
     lower, upper, inverse = wall_rows(heights, NX)
     rows = lax.broadcasted_iota(jnp.int32, (LY, NX), 0)
@@ -349,7 +351,7 @@
 
 
 def interface(
-    arrived, book, slabs, low, up, pivot, reply, value, spec, lines, top, back,
+    arrived, book, slabs, lead, gain, pivot, reply, value, spec, lines, top, back,
 ):
     dft_hi, dft_lo, idft = slabs[:128, :], slabs[128:256, :], slabs[256:, :]
     idft_hi, idft_lo = idft[:, :128], idft[:, 128:]
@@ -399,25 +401,23 @@
             right = weight * lines[z : z + 1, :]
             if z % LZ == 0:
                 right = right + top[z // LZ]
+            now = right * pivot[z]
             if s > 0:
-                if z < half:
-                    right = right + low[z : z + 1, :] * value[z - 1]
-                else:
-                    right = right + up[z : z + 1, :] * value[z + 1]
-            value[z] = right * pivot[z]
-    alpha = up[half - 1 : half, :] * pivot[half - 1]
-    beta = low[half : half + 1, :] * pivot[half]
+                now = now + lead[z] * value[z - 1 if z < half else z + 1]
+            value[z] = now
+    alpha = gain[half - 1]
+    beta = gain[half]
     below = (value[half - 1] + alpha * value[half]) / (1.0 - alpha * beta)
     above = value[half] + beta * below
     for s in range(half):
         for z in (half - 1 - s, half + s):
             if z < half:
                 if s > 0:
-                    below = value[z] + up[z : z + 1, :] * pivot[z] * below
+                    below = value[z] + gain[z] * below
                 now = below
             else:
                 if s > 0:
-                    above = value[z] + low[z : z + 1, :] * pivot[z] * above
+                    above = value[z] + gain[z] * above
                 now = above
             lines[z : z + 1, :] = jnp.sum(now * weight, axis=0, keepdims=True)
             if z % LZ == 0:
@@ -522,7 +522,7 @@
     hbm = pl.BlockSpec(memory_space=pltpu.HBM)
     params = pltpu.CompilerParams(vmem_limit_bytes=50 * 2**20)
     shape = jax.ShapeDtypeStruct
-    message, kept, heights, book, slabs, low, up, pivot, block, shared = pl.pallas_call(
+    message, kept, heights, book, slabs, low, up, pivot, block, shared, lead, gain = pl.pallas_call(
         eliminate,
         out_shape=(
             pltpu.VMEM((3 * DEV, 128), f32),
@@ -535,9 +535,11 @@
             pltpu.VMEM((NZ, GY, 128), f32),
             pltpu.VMEM((KX, (LZ - 1) * LY, 256), f32),
             pltpu.VMEM((SHARED, 256), bf16),
+            pltpu.VMEM((NZ, GY, 128), f32),
+            pltpu.VMEM((NZ, GY, 128), f32),
         ),
         in_specs=[hbm] * 6,
-        out_specs=(vmem,) * 10,
+        out_specs=(vmem,) * 12,
         scratch_shapes=[
             pltpu.SMEM((NZ,), f32),
             pltpu.VMEM((LZ, LY, NX), f32),
@@ -576,7 +578,7 @@
         ],
         compiler_params=params,
         name="interface",
-    )(near(arrived), near(book), near(slabs), near(low), near(up), near(pivot))
+    )(near(arrived), near(book), near(slabs), near(lead), near(gain), near(pivot))
     answered = trade(reply)
     return pl.pallas_call(
         restore,

time: 67.4 us -> 67.9 us (level)
  no operation moved by 1% of the time
where the time goes in v4:
time: 67.9 us; the launch traced here: 67.8 us
  blocking collectives  56.8 us (84%)
  Pallas kernels  11 us (16%)
    all_to_all x2, blocking collectives, on_device(): lax.all_to_all(x.reshape(DEV, 1, 384), axes, split_axis=0, concat_axis=0,...  56.8 us
    pallas_call x1, Pallas kernels, on_device(): pl.pallas_call(eliminate, out_shape=(pltpu.VMEM((3 * DEV, 128), f32), plt...  5.55 us
    pallas_call x1, Pallas kernels, on_device(): pl.pallas_call(interface, out_shape=pltpu.VMEM((3 * DEV, 128), f32), in_s...  2.89 us
    pallas_call x1, Pallas kernels, on_device(): pl.pallas_call(restore, out_shape=shape((LZ, LY, NX), f32), in_specs=[vme...  2.55 us

profile of v4, /device:TPU:1, one launch (start us, length us, event | category | flops | bytes accessed | tf_op | source)
XLA Modules:
  0.0 67.8 jit_solution(15752314570697361423)
XLA Ops:
  0.0 5.6 %eliminate.1 = (f32[768,128]{1,0:T(8,128)S(1)}, f32[4,256,256]{2,1,0:T(8,128)S(1)}, f32[64,128]{1,0:T(8,128)S(1)}, f32[4384,128]{1,0:T(8,128)S(1)}, bf16[512,256...) custom-call(f32[64]{0:T(128)} %spacing_in.1, ...), custom_call_target="tpu_custom_call" | custom-call | tf_op jit(solution)/shard_map/eliminate/pallas_call | solution.py:525
  5.6 33.6 %all_to_all.10 = f32[256,1,384]{2,1,0:T(1,128)S(1)} all-to-all(f32[256,1,384]{2,1,0:T(1,128)S(1)} %bitcast.7), channel_id=1, replica_groups=mesh['gz'=8,'gy'=32] {'gy','gz'}, dimensions={0} | all-to-all | bytes 786432 | tf_op jit(solution)/shard_map/all_to_all | solution.py:563
  39.2 0.0 copy-start
  39.2 2.9 %interface.1 = f32[768,128]{1,0:T(8,128)S(1)} custom-call(f32[768,128]{1,0:T(8,128)S(1)} %bitcast.5, f32[4384,128]{1,0:T(8,128)S(1)} %get-tuple-element.17.book, bf16[512,256]{1,0:T(8,128)(2,1)S(1)} %get-tuple-element.18.slabs, f32[64,32,128]{2,1,0:T(8,128)S(1)} %get-tuple-element.19.lead, f32[64,32,128]{2,1,0:T(8,128)S(1)} %get-tuple-element.20.gain, ...), custom_call_target="tpu_custom_call" | custom-call | tf_op jit(solution)/shard_map/interface/pallas_call | solution.py:567
  42.1 23.2 %all_to_all.11 = f32[256,1,384]{2,1,0:T(1,128)S(1)} all-to-all(f32[256,1,384]{2,1,0:T(1,128)S(1)} %bitcast.6), channel_id=1, replica_groups=mesh['gz'=8,'gy'=32] {'gy','gz'}, dimensions={0} | all-to-all | bytes 786432 | tf_op jit(solution)/shard_map/all_to_all | solution.py:563
  65.3 0.0 copy-done
  65.3 2.5 %restore.1 = f32[8,32,1024]{2,1,0:T(8,128)} custom-call(f32[64,128]{1,0:T(8,128)S(1)} %get-tuple-element.15.rows, f32[768,128]{1,0:T(8,128)S(1)} %bitcast.4, f32[4,256,256]{2,1,0:T(8,128)S(1)} %get-tuple-element.22.kept, bf16[944,256]{1,0:T(8,128)(2,1)S(1)} %get-tuple-element.23.shared, f32[4,224,256]{2,1,0:T(8,128)S(1)} %get-tuple-element.24.block, ...), custom_call_target="tpu_custom_call" | custom-call | tf_op jit(solution)/shard_map/restore/pallas_call | solution.py:583
Async XLA Ops:
  39.2 26.1 %copy-start = (bf16[2048,256]{1,0:T(8,128)(2,1)S(1)}, bf16[2048,256]{1,0:T(8,128)(2,1)}, u32[]{:S(2)}) copy-start(bf16[2048,256]{1,0:T(8,128)(2,1)} %constant.8.clone.pack) | copy-start | bytes 3145732

commit v5 on v3

--- a/solution.py
+++ b/solution.py
@@ -506,9 +506,13 @@
         for k, piece in ((q, whole + swing), (q + 2, whole - swing)):
             here = pl.ds(256 * k, 256)
             result[:, :, 256 * k : 256 * (k + 1)] = piece.reshape(LZ, LY, 256)
-            copy = pltpu.make_async_copy(result.at[:, :, here], pressure.at[:, :, here], out_sem.at[k])
-            copy.start()
-            copies.append(copy)
+            for part in range(2):
+                where = pl.ds(part * LZ // 2, LZ // 2)
+                copy = pltpu.make_async_copy(
+                    result.at[where, :, here], pressure.at[where, :, here], out_sem.at[2 * k + part]
+                )
+                copy.start()
+                copies.append(copy)
     for copy in copies:
         copy.wait()
 
@@ -586,7 +590,7 @@
         scratch_shapes=[
             pltpu.VMEM((384, 256), f32),
             pltpu.VMEM((LZ, LY, NX), f32),
-            pltpu.SemaphoreType.DMA((4,)),
+            pltpu.SemaphoreType.DMA((8,)),
         ],
         compiler_params=params,
         name="restore",

time: 67.4 us -> 67.4 us (level)
  no operation moved by 1% of the time
where the time goes in v5:
time: 67.4 us; the launch traced here: 67.3 us
  blocking collectives  56.8 us (84%)
  Pallas kernels  10.4 us (15%)
    all_to_all x2, blocking collectives, on_device(): lax.all_to_all(x.reshape(DEV, 1, 384), axes, split_axis=0, concat_axis=0,...  56.8 us
    pallas_call x1, Pallas kernels, on_device(): pl.pallas_call(eliminate, out_shape=(pltpu.VMEM((3 * DEV, 128), f32), plt...  4.9 us
    pallas_call x1, Pallas kernels, on_device(): pl.pallas_call(interface, out_shape=pltpu.VMEM((3 * DEV, 128), f32), in_s...  2.96 us
    pallas_call x1, Pallas kernels, on_device(): pl.pallas_call(restore, out_shape=shape((LZ, LY, NX), f32), in_specs=[vme...  2.57 us

profile of v5, /device:TPU:1, one launch (start us, length us, event | category | flops | bytes accessed | tf_op | source)
XLA Modules:
  0.0 67.3 jit_solution(16937675788130541392)
XLA Ops:
  0.0 4.9 %eliminate.1 = (f32[768,128]{1,0:T(8,128)S(1)}, f32[4,256,256]{2,1,0:T(8,128)S(1)}, f32[64,128]{1,0:T(8,128)S(1)}, f32[4384,128]{1,0:T(8,128)S(1)}, bf16[512,256...) custom-call(f32[64]{0:T(128)} %spacing_in.1, ...), custom_call_target="tpu_custom_call" | custom-call | tf_op jit(solution)/shard_map/eliminate/pallas_call | solution.py:529
  4.9 33.6 %all_to_all.10 = f32[256,1,384]{2,1,0:T(1,128)S(1)} all-to-all(f32[256,1,384]{2,1,0:T(1,128)S(1)} %bitcast.7), channel_id=1, replica_groups=mesh['gz'=8,'gy'=32] {'gy','gz'}, dimensions={0} | all-to-all | bytes 786432 | tf_op jit(solution)/shard_map/all_to_all | solution.py:565
  38.5 0.0 copy-start
  38.5 3.0 %interface.1 = f32[768,128]{1,0:T(8,128)S(1)} custom-call(f32[768,128]{1,0:T(8,128)S(1)} %bitcast.5, f32[4384,128]{1,0:T(8,128)S(1)} %get-tuple-element.17.book, bf16[512,256]{1,0:T(8,128)(2,1)S(1)} %get-tuple-element.18.slabs, f32[64,128]{1,0:T(8,128)S(1)} %get-tuple-element.19.low, f32[64,128]{1,0:T(8,128)S(1)} %get-tuple-element.20.up, ...), custom_call_target="tpu_custom_call" | custom-call | tf_op jit(solution)/shard_map/interface/pallas_call | solution.py:569
  41.5 23.2 %all_to_all.11 = f32[256,1,384]{2,1,0:T(1,128)S(1)} all-to-all(f32[256,1,384]{2,1,0:T(1,128)S(1)} %bitcast.6), channel_id=1, replica_groups=mesh['gz'=8,'gy'=32] {'gy','gz'}, dimensions={0} | all-to-all | bytes 786432 | tf_op jit(solution)/shard_map/all_to_all | solution.py:565
  64.7 0.0 copy-done
  64.7 2.6 %restore.1 = f32[8,32,1024]{2,1,0:T(8,128)} custom-call(f32[64,128]{1,0:T(8,128)S(1)} %get-tuple-element.15.rows, f32[768,128]{1,0:T(8,128)S(1)} %bitcast.4, f32[4,256,256]{2,1,0:T(8,128)S(1)} %get-tuple-element.22.kept, bf16[944,256]{1,0:T(8,128)(2,1)S(1)} %get-tuple-element.23.shared, f32[4,224,256]{2,1,0:T(8,128)S(1)} %get-tuple-element.24.block, ...), custom_call_target="tpu_custom_call" | custom-call | tf_op jit(solution)/shard_map/restore/pallas_call | solution.py:585
Async XLA Ops:
  38.5 26.2 %copy-start = (bf16[2048,256]{1,0:T(8,128)(2,1)S(1)}, bf16[2048,256]{1,0:T(8,128)(2,1)}, u32[]{:S(2)}) copy-start(bf16[2048,256]{1,0:T(8,128)(2,1)} %constant.8.clone.pack) | copy-start | bytes 3145732
